TPU v7x, 256 devices: a whole 4x4x8 slice. The times are simulated.
256 devices in a mesh: section: 2 (over x_lo), lat: 4 (over x_hi, core), lon: 32 (over y, z).
Axes of the slice: x: 4 (x_hi: 2, x_lo: 2; x = x_hi * 2 + x_lo), y: 4, z: 8, core: 2. Of those that a mesh axis runs over, the one named last changes fastest.
Arguments:
- fields: bfloat16 [2, 4, 24, 384, 384], P(None, None, 'lat', 'lon'), may hold values from -6 to 6
- surface_class: int32 [4, 24, 384], replicated, may hold values from 0 to 2
- norm_gains: bfloat16 [2, 2, 384], P('section'), may hold values from 0.25 to 1.75
- joint_proj: bfloat16 [2, 384, 1152], P('section'), may hold values from -0.3125 to 0.3125
- out_proj: bfloat16 [2, 384, 384], P('section'), may hold values from -0.3125 to 0.3125
- expand_proj: bfloat16 [2, 384, 1536], P('section'), may hold values from -0.3125 to 0.3125
- reduce_proj: bfloat16 [2, 1536, 384], P('section'), may hold values from -0.15625 to 0.15625
- earth_bias: bfloat16 [2, 8, 12, 3312], P('section'), may hold values from -4 to 300
Outputs:
- section_fields: bfloat16 [2, 2, 4, 24, 384, 384], P('section', None, None, 'lat', 'lon')
Inputs may be any that keep to these rules, and one draw needn't show every extreme that they name: `surface_class`: tokens attend only to tokens of equal class inside a window.
All inputs are finite; a program needn't handle non-finite values.
Results may differ from a plain program's by a relative error of at most 0.013.
Values may be sent and summed in bfloat16 or wider, within the bound.
A program may use at most 64 MiB of HBM per device.

v0:
```python
import jax
import jax.numpy as jnp
import numpy as np
from jax import lax
from jax.sharding import PartitionSpec as P

WIN_P = 2
WIN_H = 6
WIN_W = 12


def from_behind(value, axis, steps):
    count = lax.axis_size(axis)
    pairs = [(source, (source + steps) % count) for source in range(count)]
    return lax.ppermute(value, axis, pairs)


def shifted(block, axis, distance):
    devices = range(lax.axis_size(axis))
    route = [(i - distance, i) for i in devices if i - distance in devices]
    return lax.ppermute(block, axis, route)


def relative_index():
    level_grid, row_grid, col_grid = np.meshgrid(
        np.arange(WIN_P), np.arange(WIN_H), np.arange(WIN_W), indexing="ij"
    )
    level_flat = level_grid.reshape(-1)
    row_flat = row_grid.reshape(-1)
    col_flat = col_grid.reshape(-1)
    level_part = level_flat[:, None] + level_flat[None, :] * WIN_P
    row_part = row_flat[:, None] + row_flat[None, :] * WIN_H
    col_part = col_flat[:, None] - col_flat[None, :] + WIN_W - 1
    joined = level_part * (WIN_H * WIN_H * (2 * WIN_W - 1)) + row_part * (2 * WIN_W - 1) + col_part
    return joined.astype(np.int32)


def layer_norm(values, gain):
    average = jnp.mean(values, axis=-1, keepdims=True)
    centred = values - average
    spread = jnp.mean(centred * centred, axis=-1, keepdims=True)
    return centred * lax.rsqrt(spread + 1e-05) * gain.astype(jnp.float32)


def to_windows(token_grid):
    level_count, row_count, col_count = token_grid.shape[:3]
    trailing = token_grid.shape[3:]
    shaped = token_grid.reshape(
        (level_count // WIN_P, WIN_P, row_count // WIN_H, WIN_H, col_count // WIN_W, WIN_W)
        + trailing
    )
    order = (0, 2, 4, 1, 3, 5) + tuple(range(6, 6 + len(trailing)))
    return shaped.transpose(order).reshape((-1, WIN_P * WIN_H * WIN_W) + trailing)


def from_windows(windowed, level_count, row_count, col_count):
    trailing = windowed.shape[2:]
    shaped = windowed.reshape(
        (level_count // WIN_P, row_count // WIN_H, col_count // WIN_W, WIN_P, WIN_H, WIN_W)
        + trailing
    )
    order = (0, 3, 1, 4, 2, 5) + tuple(range(6, 6 + len(trailing)))
    return shaped.transpose(order).reshape((level_count, row_count, col_count) + trailing)


def window_core(window_tokens, region_win, bias_win, params):
    gain_pair, joint_weight, output_weight, expand_weight, reduce_weight = params
    window_count, window_size, model_width = window_tokens.shape
    head_count = bias_win.shape[1]
    head_size = model_width // head_count
    flat_rows = window_tokens.reshape((-1, model_width))
    hidden_start = flat_rows.astype(jnp.float32)
    normed = layer_norm(hidden_start, gain_pair[0]).astype(jnp.bfloat16)
    projected = jnp.dot(normed, joint_weight, preferred_element_type=jnp.float32).astype(
        jnp.bfloat16
    )
    projected = projected.reshape((window_count, window_size, 3, head_count, head_size))
    scores = jnp.einsum(
        "wqhd,wkhd->whqk",
        projected[:, :, 0],
        projected[:, :, 1],
        preferred_element_type=jnp.float32,
    )
    scores = scores * head_size ** (-0.5) + bias_win.astype(jnp.float32)
    same_region = region_win[:, :, None] == region_win[:, None, :]
    scores = jnp.where(same_region[:, None], scores, -1e30)
    row_max = jnp.max(scores, axis=-1, keepdims=True)
    exponent = jnp.exp(scores - row_max)
    attn_weights = (exponent / jnp.sum(exponent, axis=-1, keepdims=True)).astype(jnp.bfloat16)
    mixed_heads = jnp.einsum(
        "whqk,wkhd->wqhd", attn_weights, projected[:, :, 2], preferred_element_type=jnp.float32
    )
    mixed_heads = mixed_heads.astype(jnp.bfloat16).reshape((-1, model_width))
    hidden = hidden_start + jnp.dot(mixed_heads, output_weight, preferred_element_type=jnp.float32)
    normed_again = layer_norm(hidden, gain_pair[1]).astype(jnp.bfloat16)
    activated = jax.nn.gelu(
        jnp.dot(normed_again, expand_weight, preferred_element_type=jnp.float32), approximate=False
    ).astype(jnp.bfloat16)
    result = (
        hidden + jnp.dot(activated, reduce_weight, preferred_element_type=jnp.float32)
    ).astype(jnp.bfloat16)
    return result.reshape((window_count, window_size, model_width))


def local_block(token_grid, region_grid, kind_grid, params, bias_grid):
    level_count, row_count, col_count, model_width = token_grid.shape
    bias_win = jnp.take(bias_grid, kind_grid.reshape(-1), axis=0)
    processed = window_core(to_windows(token_grid), to_windows(region_grid), bias_win, params)
    return from_windows(processed, level_count, row_count, col_count)


def roll_forward(token_grid):
    level_shift = WIN_P // 2
    row_shift = WIN_H // 2
    col_shift = WIN_W // 2
    turned = jnp.roll(token_grid, -level_shift, axis=0)
    row_cells = from_behind(turned[:, :row_shift], "lat", -1)
    turned = jnp.concatenate([turned[:, row_shift:], row_cells], axis=1)
    col_cells = from_behind(turned[:, :, :col_shift], "lon", -1)
    return jnp.concatenate([turned[:, :, col_shift:], col_cells], axis=2)


def return_cells(token_grid):
    row_shift = WIN_H // 2
    col_shift = WIN_W // 2
    col_count = token_grid.shape[2]
    row_count = token_grid.shape[1]
    col_cells = from_behind(token_grid[:, :, col_count - col_shift :], "lon", 1)
    turned = jnp.concatenate([col_cells, token_grid[:, :, : col_count - col_shift]], axis=2)
    row_cells = from_behind(turned[:, row_count - row_shift :], "lat", 1)
    return jnp.concatenate([row_cells, turned[:, : row_count - row_shift]], axis=1)


def body(
    fields, surface_class, norm_gains, joint_proj, out_proj, expand_proj, reduce_proj, earth_bias
):
    section_index = lax.axis_index("section")
    micro_count, level_count, row_count, col_count, model_width = fields.shape
    row_start = lax.axis_index("lat") * row_count
    col_start = lax.axis_index("lon") * col_count
    level_start = jnp.zeros((), jnp.int32)
    total_rows = row_count * lax.axis_size("lat")
    shifts = (-(WIN_P // 2), -(WIN_H // 2), -(WIN_W // 2))
    block_shape = (level_count, row_count, col_count)
    rolled_class = lax.dynamic_slice(
        jnp.roll(surface_class, shifts, axis=(0, 1, 2)),
        (level_start, row_start, col_start),
        block_shape,
    )
    plain_class = lax.dynamic_slice(surface_class, (level_start, row_start, col_start), block_shape)
    level_flag = (jnp.arange(level_count) >= level_count - WIN_P // 2).astype(jnp.int32)
    row_flag = (row_start + jnp.arange(row_count) >= total_rows - WIN_H // 2).astype(jnp.int32)
    first_regions = rolled_class * 4 + level_flag[:, None, None] * 2 + row_flag[None, :, None]
    second_regions = plain_class * 4
    level_wins = jnp.arange(level_count // WIN_P, dtype=jnp.int32)
    local_rows = jnp.arange(row_count // WIN_H, dtype=jnp.int32)
    own_kinds = (
        level_wins[:, None] * (total_rows // WIN_H) + row_start // WIN_H + local_rows[None, :]
    ).reshape(-1)
    kind_grid = level_wins[:, None, None] * (row_count // WIN_H) + local_rows[None, :, None]
    relative = jnp.asarray(relative_index())
    is_first = section_index == 0
    own_params = tuple(
        (member[0] for member in (norm_gains, joint_proj, out_proj, expand_proj, reduce_proj))
    )
    bias_grid = jnp.take(earth_bias[0], own_kinds, axis=0)[:, :, relative]
    regions_mine = jnp.where(is_first, first_regions, second_regions)
    half_levels = level_count // 2
    half_wins = half_levels // WIN_P
    received = jnp.zeros_like(fields[0])
    results = []
    for step_index in range(micro_count + 1):
        current = jnp.where(is_first, fields[min(step_index, micro_count - 1)], received)
        token_grid = jnp.where(is_first, roll_forward(current), current)
        halves = []
        for half_index in range(2):
            piece = token_grid[half_index * half_levels : (half_index + 1) * half_levels]
            region_piece = regions_mine[half_index * half_levels : (half_index + 1) * half_levels]
            kind_piece = kind_grid[half_index * half_wins : (half_index + 1) * half_wins]
            done = local_block(piece, region_piece, kind_piece, own_params, bias_grid)
            halves.append(jnp.where(is_first, return_cells(done), done))
        combined = jnp.concatenate(halves, axis=0)
        result = jnp.where(is_first, jnp.roll(combined, WIN_P // 2, axis=0), combined)
        results.append(result)
        if step_index < micro_count:
            received = shifted(result, "section", 1)
    ordered = [
        jnp.where(is_first, results[micro_index], results[micro_index + 1])
        for micro_index in range(micro_count)
    ]
    return jnp.stack(ordered)[None]


def solution(mesh):
    return jax.shard_map(
        body,
        mesh=mesh,
        in_specs=(
            P(None, None, "lat", "lon", None),
            P(),
            P("section", None, None),
            P("section", None, None),
            P("section", None, None),
            P("section", None, None),
            P("section", None, None),
            P("section", None, None, None),
        ),
        out_specs=P("section", None, None, "lat", "lon", None),
        check_vma=False,
    )
```

profile of v0, /device:TPU:2, one launch (start us, length us, event | category | flops | bytes accessed | tf_op | source)
XLA Modules:
  0.0 263.1 jit_solution(3401567255251952362)
XLA Ops:
  0.0 2.0 fusion.617
  8.1 2.3 copy.66
  10.5 51.2 %gather_fusion.1 = bf16[20736,2,12]{2,1,0:T(2,128)(2,1)} fusion(bf16[2,12,3312]{1,0,2:T(2,128)(2,1)S(1)} %copy.66, s32[21504]{0:T(1024)S(1)} %pad_clamp_fusion), kind=kCustom, calls=%fused_computation.1 | custom fusion | bytes 2073600 | tf_op jit(solution)/shard_map/gather | solution.py:166
  61.7 28.8 %copy.68 = bf16[144,144,2,12]{0,1,3,2:T(8,128)(2,1)} copy(bf16[144,144,2,12]{3,2,1,0:T(2,128)(2,1)} %bitcast.303) | data formatting | bytes 1990656 | tf_op jit(solution)/shard_map/gather | solution.py:166
  91.5 8.8 %collective-permute-start.1 = (bf16[4,6,6,384]{3,2,1,0:T(8,128)(2,1)S(1)}, bf16[4,6,6,384]{3,2,1,0:T(8,128)(2,1)S(1)}, u32[]{:S(2)}, u32[]{:S(2)}) collective-permute-start(bf16[4,6,6,384]{3,2,1,0:T(8,128)(2,1)S(1)} %get-tuple-element.64), channel_id=1, source_target_pairs={{0,31},{1,0},{2,1},{3,2},{4,3},{5,4},{6,5},{7,6},{8,7},{9,8},{10,9... | collective-permute-start | bytes 331784 | tf_op jit(solution)/shard_map/ppermute | solution.py:15
  100.4 2.7 %collective-permute-done.1 = bf16[4,6,6,384]{3,2,1,0:T(8,128)(2,1)S(1)} collective-permute-done((bf16[4,6,6,384]{3,2,1,0:T(8,128)(2,1)S(1)}, bf16[4,6,6,384]{3,2,1,0:T(8,128)(2,1)S(1)}, u32[]{:S(2)}, u32[]{:S(2)}) %collective-permute-start.1) | collective-permute-done | bytes 110624 | tf_op jit(solution)/shard_map/ppermute | solution.py:15
  105.6 2.0 fusion.625
  110.0 3.8 %fusion.66 = bf16[144,384]{1,0:T(8,128)(2,1)S(1)} fusion(f32[144,384]{1,0:T(8,128)S(1)} %get-tuple-element.88, bf16[1,1536,384]{2,1,0:T(8,128)(2,1)S(1)} %copy-done, bf16[1,384,1536]{2,1,0:T(8,128)(2,1)} %param.16, f32[144]{0:T(256)S(1)} %add_rsqrt_fusion.10, f32[144]{0:T(256)S(1)} %broadcast_multiply_fusion.10, f32[384]{0:T(512)S(1)} %get-tuple-element.29), kind=kOutput, calls=%fused_computation.86 | convolution fusion | flops 354447360 | bytes 2693760 | tf_op jit(solution)/shard_map/dot_general | solution.py:100
  115.3 2.0 fusion.627
  119.6 3.8 %fusion.69 = bf16[144,384]{1,0:T(8,128)(2,1)S(1)} fusion(f32[144,384]{1,0:T(8,128)S(1)} %get-tuple-element.92, bf16[1,1536,384]{2,1,0:T(8,128)(2,1)S(1)} %copy-done, bf16[1,384,1536]{2,1,0:T(8,128)(2,1)} %param.16, f32[384]{0:T(512)S(1)} %get-tuple-element.29, f32[144]{0:T(256)S(1)} %add_rsqrt_fusion.11, f32[144]{0:T(256)S(1)} %broadcast_multiply_fusion.11), kind=kOutput, calls=%fused_computation.87 | convolution fusion | flops 354447360 | bytes 2693760 | tf_op jit(solution)/shard_map/dot_general | solution.py:100
  123.7 8.0 %collective-permute-done.2 = bf16[2,6,6,384]{3,2,1,0:T(8,128)(2,1)S(1)} collective-permute-done((bf16[2,6,6,384]{3,2,1,0:T(8,128)(2,1)S(1)}, bf16[2,6,6,384]{3,2,1,0:T(8,128)(2,1)S(1)}, u32[]{:S(2)}, u32[]{:S(2)}) %collective-permute-start.2) | collective-permute-done | bytes 55328 | tf_op jit(solution)/shard_map/ppermute | solution.py:15
  133.9 3.4 %collective-permute-done.3 = bf16[2,3,12,384]{3,2,1,0:T(8,128)(2,1)S(1)} collective-permute-done((bf16[2,3,12,384]{3,2,1,0:T(8,128)(2,1)S(1)}, bf16[2,3,12,384]{3,2,1,0:T(8,128)(2,1)S(1)}, u32[]{:S(2)}, u32[]{:S(2)}) %collective-permute-start.3) | collective-permute-done | bytes 55328 | tf_op jit(solution)/shard_map/ppermute | solution.py:15
  139.6 7.3 %collective-permute-done.6 = bf16[4,6,12,384]{3,2,1,0:T(8,128)(2,1)S(1)} collective-permute-done((bf16[4,6,12,384]{3,2,1,0:T(8,128)(2,1)S(1)}, bf16[4,6,12,384]{3,2,1,0:T(8,128)(2,1)S(1)}, u32[]{:S(2)}, u32[]{:S(2)}) %collective-permute-start.6) | collective-permute-done | bytes 221216 | tf_op jit(solution)/shard_map/ppermute | solution.py:21
  147.2 2.7 %collective-permute-done.7 = bf16[4,3,12,384]{3,2,1,0:T(8,128)(2,1)S(1)} collective-permute-done((bf16[4,3,12,384]{3,2,1,0:T(8,128)(2,1)S(1)}, bf16[4,3,12,384]{3,2,1,0:T(8,128)(2,1)S(1)}, u32[]{:S(2)}, u32[]{:S(2)}) %collective-permute-start.7) | collective-permute-done | bytes 110624 | tf_op jit(solution)/shard_map/ppermute | solution.py:15
  149.9 2.1 collective-permute-start.8
  152.0 3.5 %collective-permute-done.8 = bf16[4,6,6,384]{3,2,1,0:T(8,128)(2,1)S(1)} collective-permute-done((bf16[4,6,6,384]{3,2,1,0:T(8,128)(2,1)S(1)}, bf16[4,6,6,384]{3,2,1,0:T(8,128)(2,1)S(1)}, u32[]{:S(2)}, u32[]{:S(2)}) %collective-permute-start.8) | collective-permute-done | bytes 110624 | tf_op jit(solution)/shard_map/ppermute | solution.py:15
  160.0 2.0 copy.73
  162.0 2.0 fusion.629
  166.9 4.6 %fusion.63 = bf16[144,384]{1,0:T(8,128)(2,1)} fusion(f32[144,384]{1,0:T(8,128)} %copy-done.9, bf16[1,1536,384]{2,1,0:T(8,128)(2,1)S(1)} %copy-done, bf16[1,384,1536]{2,1,0:T(8,128)(2,1)} %param.16, f32[144]{0:T(256)S(1)} %add_rsqrt_fusion.9, f32[144]{0:T(256)S(1)} %broadcast_multiply_fusion.9, f32[384]{0:T(512)S(1)} %get-tuple-element.29), kind=kOutput, calls=%fused_computation.85 | convolution fusion | flops 354447360 | bytes 2693760 | tf_op jit(solution)/shard_map/dot_general | solution.py:100
  181.4 3.8 %fusion.60 = bf16[144,384]{1,0:T(8,128)(2,1)S(1)} fusion(f32[144,384]{1,0:T(8,128)S(1)} %get-tuple-element.36, bf16[1,1536,384]{2,1,0:T(8,128)(2,1)S(1)} %copy-done, bf16[1,384,1536]{2,1,0:T(8,128)(2,1)} %param.16, f32[144]{0:T(256)S(1)} %add_rsqrt_fusion.8, f32[144]{0:T(256)S(1)} %broadcast_multiply_fusion.8, f32[384]{0:T(512)S(1)} %get-tuple-element.29), kind=kOutput, calls=%fused_computation.84 | convolution fusion | flops 354447360 | bytes 2693760 | tf_op jit(solution)/shard_map/dot_general | solution.py:100
  187.3 6.3 %collective-permute-done.11 = bf16[2,6,6,384]{3,2,1,0:T(8,128)(2,1)S(1)} collective-permute-done((bf16[2,6,6,384]{3,2,1,0:T(8,128)(2,1)S(1)}, bf16[2,6,6,384]{3,2,1,0:T(8,128)(2,1)S(1)}, u32[]{:S(2)}, u32[]{:S(2)}) %collective-permute-start.11) | collective-permute-done | bytes 55328 | tf_op jit(solution)/shard_map/ppermute | solution.py:15
  194.6 4.3 %collective-permute-done.12 = bf16[2,3,12,384]{3,2,1,0:T(8,128)(2,1)S(1)} collective-permute-done((bf16[2,3,12,384]{3,2,1,0:T(8,128)(2,1)S(1)}, bf16[2,3,12,384]{3,2,1,0:T(8,128)(2,1)S(1)}, u32[]{:S(2)}, u32[]{:S(2)}) %collective-permute-start.12) | collective-permute-done | bytes 55328 | tf_op jit(solution)/shard_map/ppermute | solution.py:15
  200.5 8.0 %collective-permute-done.13 = bf16[4,6,12,384]{3,2,1,0:T(8,128)(2,1)S(1)} collective-permute-done((bf16[4,6,12,384]{3,2,1,0:T(8,128)(2,1)S(1)}, bf16[4,6,12,384]{3,2,1,0:T(8,128)(2,1)S(1)}, u32[]{:S(2)}, u32[]{:S(2)}) %collective-permute-start.13) | collective-permute-done | bytes 221216 | tf_op jit(solution)/shard_map/ppermute | solution.py:21
  208.8 2.7 %collective-permute-done.14 = bf16[4,3,12,384]{3,2,1,0:T(8,128)(2,1)S(1)} collective-permute-done((bf16[4,3,12,384]{3,2,1,0:T(8,128)(2,1)S(1)}, bf16[4,3,12,384]{3,2,1,0:T(8,128)(2,1)S(1)}, u32[]{:S(2)}, u32[]{:S(2)}) %collective-permute-start.14) | collective-permute-done | bytes 110624 | tf_op jit(solution)/shard_map/ppermute | solution.py:15
  211.5 2.3 collective-permute-start.15
  213.8 4.0 %collective-permute-done.15 = bf16[4,6,6,384]{3,2,1,0:T(8,128)(2,1)S(1)} collective-permute-done((bf16[4,6,6,384]{3,2,1,0:T(8,128)(2,1)S(1)}, bf16[4,6,6,384]{3,2,1,0:T(8,128)(2,1)S(1)}, u32[]{:S(2)}, u32[]{:S(2)}) %collective-permute-start.15) | collective-permute-done | bytes 110624 | tf_op jit(solution)/shard_map/ppermute | solution.py:15
  227.0 2.0 fusion.632
  239.4 3.8 %fusion.57 = bf16[144,384]{1,0:T(8,128)(2,1)S(1)} fusion(f32[144,384]{1,0:T(8,128)S(1)} %get-tuple-element.102, bf16[1,1536,384]{2,1,0:T(8,128)(2,1)S(1)} %copy-done, bf16[1,384,1536]{2,1,0:T(8,128)(2,1)} %param.16, f32[144]{0:T(256)S(1)} %add_rsqrt_fusion.7, f32[144]{0:T(256)S(1)} %broadcast_multiply_fusion.7, f32[384]{0:T(512)S(1)} %get-tuple-element.29), kind=kOutput, calls=%fused_computation.83 | convolution fusion | flops 354447360 | bytes 2693760 | tf_op jit(solution)/shard_map/dot_general | solution.py:100
  243.5 3.8 %fusion.54 = bf16[144,384]{1,0:T(8,128)(2,1)S(1)} fusion(f32[144,384]{1,0:T(8,128)S(1)} %get-tuple-element.32, bf16[1,1536,384]{2,1,0:T(8,128)(2,1)S(1)} %copy-done, bf16[1,384,1536]{2,1,0:T(8,128)(2,1)} %param.16, f32[144]{0:T(256)S(1)} %add_rsqrt_fusion.6, f32[144]{0:T(256)S(1)} %broadcast_multiply_fusion.6, f32[384]{0:T(512)S(1)} %get-tuple-element.29), kind=kOutput, calls=%fused_computation.82 | convolution fusion | flops 354447360 | bytes 2693760 | tf_op jit(solution)/shard_map/dot_general | solution.py:100
  247.5 4.1 %collective-permute-done.16 = bf16[2,6,6,384]{3,2,1,0:T(8,128)(2,1)S(1)} collective-permute-done((bf16[2,6,6,384]{3,2,1,0:T(8,128)(2,1)S(1)}, bf16[2,6,6,384]{3,2,1,0:T(8,128)(2,1)S(1)}, u32[]{:S(2)}, u32[]{:S(2)}) %collective-permute-start.16) | collective-permute-done | bytes 55328 | tf_op jit(solution)/shard_map/ppermute | solution.py:15
  251.8 4.1 %collective-permute-done.18 = bf16[2,6,6,384]{3,2,1,0:T(8,128)(2,1)S(1)} collective-permute-done((bf16[2,6,6,384]{3,2,1,0:T(8,128)(2,1)S(1)}, bf16[2,6,6,384]{3,2,1,0:T(8,128)(2,1)S(1)}, u32[]{:S(2)}, u32[]{:S(2)}) %collective-permute-start.18) | collective-permute-done | bytes 55328 | tf_op jit(solution)/shard_map/ppermute | solution.py:15
  257.1 4.1 %collective-permute-done.19 = bf16[2,3,12,384]{3,2,1,0:T(8,128)(2,1)S(1)} collective-permute-done((bf16[2,3,12,384]{3,2,1,0:T(8,128)(2,1)S(1)}, bf16[2,3,12,384]{3,2,1,0:T(8,128)(2,1)S(1)}, u32[]{:S(2)}, u32[]{:S(2)}) %collective-permute-start.19) | collective-permute-done | bytes 55328 | tf_op jit(solution)/shard_map/ppermute | solution.py:15
  (236 shorter events, 65.4 us)
Async XLA Ops:
  0.0 110.0 %copy-start = (bf16[1,1536,384]{2,1,0:T(8,128)(2,1)S(1)}, bf16[1,1536,384]{2,1,0:T(8,128)(2,1)}, u32[]{:S(2)}) copy-start(bf16[1,1536,384]{2,1,0:T(8,128)(2,1)} %param.17) | copy-start | bytes 3538948
  0.0 4.5 %copy-start.17 = (s32[4,24,384]{2,1,0:T(8,128)S(1)}, s32[4,24,384]{2,1,0:T(8,128)}, u32[]{:S(2)}) copy-start(s32[4,24,384]{2,1,0:T(8,128)} %param.12) | copy-start | bytes 442372
  0.0 4.7 %copy-start.15 = (bf16[1,8,12,3312]{3,1,2,0:T(8,128)(2,1)S(1)}, bf16[1,8,12,3312]{3,1,2,0:T(8,128)(2,1)}, u32[]{:S(2)}) copy-start(bf16[1,8,12,3312]{3,1,2,0:T(8,128)(2,1)} %param.18) | copy-start | bytes 1907716
  2.9 87.6 %collective-permute-start = (bf16[4,3,12,384]{3,2,1,0:T(8,128)(2,1)}, bf16[4,3,12,384]{3,2,1,0:T(8,128)(2,1)}, u32[]{:S(2)}, u32[]{:S(2)}) collective-permute-start(bf16[4,3,12,384]{3,2,1,0:T(8,128)(2,1)} %get-tuple-element.66), channel_id=1, source_target_pairs={{0,96},{32,0},{64,32},{96,64},{1,97},{33,1},{65,33},{97,65},{2,98}... | collective-permute-start | bytes 331784 | tf_op jit(solution)/shard_map/ppermute | solution.py:15
  61.7 38.7 %copy-start.23 = (bf16[1,2,384]{2,1,0:T(2,128)(2,1)S(1)}, bf16[1,2,384]{2,1,0:T(2,128)(2,1)}, u32[]{:S(2)}) copy-start(bf16[1,2,384]{2,1,0:T(2,128)(2,1)} %param.13) | copy-start | bytes 4612
  91.5 11.5 %collective-permute-start.1 = (bf16[4,6,6,384]{3,2,1,0:T(8,128)(2,1)S(1)}, bf16[4,6,6,384]{3,2,1,0:T(8,128)(2,1)S(1)}, u32[]{:S(2)}, u32[]{:S(2)}) collective-permute-start(bf16[4,6,6,384]{3,2,1,0:T(8,128)(2,1)S(1)} %get-tuple-element.64), channel_id=1, source_target_pairs={{0,31},{1,0},{2,1},{3,2},{4,3},{5,4},{6,5},{7,6},{8,7},{9,8},{10,9... | collective-permute-start | bytes 331784 | tf_op jit(solution)/shard_map/ppermute | solution.py:15
  123.5 23.5 %copy-start.5 = (bf16[1,4,6,12,384]{4,1,3,2,0:T(4,128)(2,1)S(1)}, bf16[1,4,6,12,384]{4,1,3,2,0:T(4,128)(2,1)}, u32[]{:S(2)}) copy-start(bf16[1,4,6,12,384]{4,1,3,2,0:T(4,128)(2,1)} %get-tuple-element.41) | copy-start | bytes 663556
  123.5 8.2 %collective-permute-start.2 = (bf16[2,6,6,384]{3,2,1,0:T(8,128)(2,1)S(1)}, bf16[2,6,6,384]{3,2,1,0:T(8,128)(2,1)S(1)}, u32[]{:S(2)}, u32[]{:S(2)}) collective-permute-start(bf16[2,6,6,384]{3,2,1,0:T(8,128)(2,1)S(1)} %get-tuple-element.81), channel_id=1, source_target_pairs={{0,1},{1,2},{2,3},{3,4},{4,5},{5,6},{6,7},{7,8},{8,9},{9,10},{10,1... | collective-permute-start | bytes 165896 | tf_op jit(solution)/shard_map/ppermute | solution.py:15
  123.6 8.9 %collective-permute-start.4 = (bf16[2,6,6,384]{3,2,1,0:T(8,128)(2,1)S(1)}, bf16[2,6,6,384]{3,2,1,0:T(8,128)(2,1)S(1)}, u32[]{:S(2)}, u32[]{:S(2)}) collective-permute-start(bf16[2,6,6,384]{3,2,1,0:T(8,128)(2,1)S(1)} %get-tuple-element.79), channel_id=1, source_target_pairs={{0,1},{1,2},{2,3},{3,4},{4,5},{5,6},{6,7},{7,8},{8,9},{9,10},{10,1... | collective-permute-start | bytes 165896 | tf_op jit(solution)/shard_map/ppermute | solution.py:15
  131.7 5.5 %collective-permute-start.3 = (bf16[2,3,12,384]{3,2,1,0:T(8,128)(2,1)S(1)}, bf16[2,3,12,384]{3,2,1,0:T(8,128)(2,1)S(1)}, u32[]{:S(2)}, u32[]{:S(2)}) collective-permute-start(bf16[2,3,12,384]{3,2,1,0:T(8,128)(2,1)S(1)} %fusion.426), channel_id=1, source_target_pairs={{0,32},{32,64},{64,96},{96,0},{1,33},{33,65},{65,97},{97,1},{2,34}... | collective-permute-start | bytes 165896 | tf_op jit(solution)/shard_map/ppermute | solution.py:15
  132.5 5.5 %collective-permute-start.5 = (bf16[2,3,12,384]{3,2,1,0:T(8,128)(2,1)S(1)}, bf16[2,3,12,384]{3,2,1,0:T(8,128)(2,1)S(1)}, u32[]{:S(2)}, u32[]{:S(2)}) collective-permute-start(bf16[2,3,12,384]{3,2,1,0:T(8,128)(2,1)S(1)} %fusion.425), channel_id=1, source_target_pairs={{0,32},{32,64},{64,96},{96,0},{1,33},{33,65},{65,97},{97,1},{2,34}... | collective-permute-start | bytes 165896 | tf_op jit(solution)/shard_map/ppermute | solution.py:15
  138.3 8.6 %collective-permute-start.6 = (bf16[4,6,12,384]{3,2,1,0:T(8,128)(2,1)S(1)}, bf16[4,6,12,384]{3,2,1,0:T(8,128)(2,1)S(1)}, u32[]{:S(2)}, u32[]{:S(2)}) collective-permute-start(bf16[4,6,12,384]{3,2,1,0:T(8,128)(2,1)S(1)} %fusion.349), channel_id=1, source_target_pairs={{0,128},{1,129},{2,130},{3,131},{4,132},{5,133},{6,134},{7,135},{8... | collective-permute-start | bytes 663560 | tf_op jit(solution)/shard_map/ppermute | solution.py:21
  147.1 2.8 %collective-permute-start.7 = (bf16[4,3,12,384]{3,2,1,0:T(8,128)(2,1)S(1)}, bf16[4,3,12,384]{3,2,1,0:T(8,128)(2,1)S(1)}, u32[]{:S(2)}, u32[]{:S(2)}) collective-permute-start(bf16[4,3,12,384]{3,2,1,0:T(8,128)(2,1)S(1)} %get-tuple-element.60), channel_id=1, source_target_pairs={{0,96},{32,0},{64,32},{96,64},{1,97},{33,1},{65,33},{97,65},{2,98}... | collective-permute-start | bytes 331784 | tf_op jit(solution)/shard_map/ppermute | solution.py:15
  149.9 5.6 %collective-permute-start.8 = (bf16[4,6,6,384]{3,2,1,0:T(8,128)(2,1)S(1)}, bf16[4,6,6,384]{3,2,1,0:T(8,128)(2,1)S(1)}, u32[]{:S(2)}, u32[]{:S(2)}) collective-permute-start(bf16[4,6,6,384]{3,2,1,0:T(8,128)(2,1)S(1)} %get-tuple-element.58), channel_id=1, source_target_pairs={{0,31},{1,0},{2,1},{3,2},{4,3},{5,4},{6,5},{7,6},{8,7},{9,8},{10,9... | collective-permute-start | bytes 331784 | tf_op jit(solution)/shard_map/ppermute | solution.py:15
  166.9 6.4 %copy-start.7 = (f32[2,6,12,384]{3,2,1,0:T(8,128)S(1)}, f32[2,6,12,384]{3,2,1,0:T(8,128)}, u32[]{:S(2)}) copy-start(f32[2,6,12,384]{3,2,1,0:T(8,128)} %get-tuple-element.55) | copy-start | bytes 663556
  173.0 12.4 %collective-permute-start.9 = (bf16[2,6,6,384]{3,2,1,0:T(8,128)(2,1)}, bf16[2,6,6,384]{3,2,1,0:T(8,128)(2,1)}, u32[]{:S(2)}, u32[]{:S(2)}) collective-permute-start(bf16[2,6,6,384]{3,2,1,0:T(8,128)(2,1)} %get-tuple-element.77), channel_id=1, source_target_pairs={{0,1},{1,2},{2,3},{3,4},{4,5},{5,6},{6,7},{7,8},{8,9},{9,10},{10,1... | collective-permute-start | bytes 165896 | tf_op jit(solution)/shard_map/ppermute | solution.py:15
  185.3 23.2 %copy-start.6 = (bf16[1,4,6,12,384]{4,1,3,2,0:T(4,128)(2,1)S(1)}, bf16[1,4,6,12,384]{4,1,3,2,0:T(4,128)(2,1)}, u32[]{:S(2)}) copy-start(bf16[1,4,6,12,384]{4,1,3,2,0:T(4,128)(2,1)} %get-tuple-element.41) | copy-start | bytes 663556
  185.3 8.2 %collective-permute-start.11 = (bf16[2,6,6,384]{3,2,1,0:T(8,128)(2,1)S(1)}, bf16[2,6,6,384]{3,2,1,0:T(8,128)(2,1)S(1)}, u32[]{:S(2)}, u32[]{:S(2)}) collective-permute-start(bf16[2,6,6,384]{3,2,1,0:T(8,128)(2,1)S(1)} %get-tuple-element.75), channel_id=1, source_target_pairs={{0,1},{1,2},{2,3},{3,4},{4,5},{5,6},{6,7},{7,8},{8,9},{9,10},{10,1... | collective-permute-start | bytes 165896 | tf_op jit(solution)/shard_map/ppermute | solution.py:15
  186.2 7.6 %collective-permute-start.10 = (bf16[2,3,12,384]{3,2,1,0:T(8,128)(2,1)S(1)}, bf16[2,3,12,384]{3,2,1,0:T(8,128)(2,1)S(1)}, u32[]{:S(2)}, u32[]{:S(2)}) collective-permute-start(bf16[2,3,12,384]{3,2,1,0:T(8,128)(2,1)S(1)} %fusion.424), channel_id=1, source_target_pairs={{0,32},{32,64},{64,96},{96,0},{1,33},{33,65},{65,97},{97,1},{2,34}... | collective-permute-start | bytes 165896 | tf_op jit(solution)/shard_map/ppermute | solution.py:15
  193.6 5.4 %collective-permute-start.12 = (bf16[2,3,12,384]{3,2,1,0:T(8,128)(2,1)S(1)}, bf16[2,3,12,384]{3,2,1,0:T(8,128)(2,1)S(1)}, u32[]{:S(2)}, u32[]{:S(2)}) collective-permute-start(bf16[2,3,12,384]{3,2,1,0:T(8,128)(2,1)S(1)} %fusion.423), channel_id=1, source_target_pairs={{0,32},{32,64},{64,96},{96,0},{1,33},{33,65},{65,97},{97,1},{2,34}... | collective-permute-start | bytes 165896 | tf_op jit(solution)/shard_map/ppermute | solution.py:15
  199.1 18.7 %copy-start.3 = (bf16[3,6,12,384]{3,2,1,0:T(8,128)(2,1)}, bf16[3,6,12,384]{3,2,1,0:T(8,128)(2,1)S(1)}, u32[]{:S(2)}) copy-start(bf16[3,6,12,384]{3,2,1,0:T(8,128)(2,1)S(1)} %fusion.364) | copy-start | bytes 497668
  199.2 9.3 %collective-permute-start.13 = (bf16[4,6,12,384]{3,2,1,0:T(8,128)(2,1)S(1)}, bf16[4,6,12,384]{3,2,1,0:T(8,128)(2,1)S(1)}, u32[]{:S(2)}, u32[]{:S(2)}) collective-permute-start(bf16[4,6,12,384]{3,2,1,0:T(8,128)(2,1)S(1)} %fusion.348), channel_id=1, source_target_pairs={{0,128},{1,129},{2,130},{3,131},{4,132},{5,133},{6,134},{7,135},{8... | collective-permute-start | bytes 663560 | tf_op jit(solution)/shard_map/ppermute | solution.py:21
  208.7 2.8 %collective-permute-start.14 = (bf16[4,3,12,384]{3,2,1,0:T(8,128)(2,1)S(1)}, bf16[4,3,12,384]{3,2,1,0:T(8,128)(2,1)S(1)}, u32[]{:S(2)}, u32[]{:S(2)}) collective-permute-start(bf16[4,3,12,384]{3,2,1,0:T(8,128)(2,1)S(1)} %get-tuple-element.54), channel_id=1, source_target_pairs={{0,96},{32,0},{64,32},{96,64},{1,97},{33,1},{65,33},{97,65},{2,98}... | collective-permute-start | bytes 331784 | tf_op jit(solution)/shard_map/ppermute | solution.py:15
  211.5 6.2 %collective-permute-start.15 = (bf16[4,6,6,384]{3,2,1,0:T(8,128)(2,1)S(1)}, bf16[4,6,6,384]{3,2,1,0:T(8,128)(2,1)S(1)}, u32[]{:S(2)}, u32[]{:S(2)}) collective-permute-start(bf16[4,6,6,384]{3,2,1,0:T(8,128)(2,1)S(1)} %get-tuple-element.52), channel_id=1, source_target_pairs={{0,31},{1,0},{2,1},{3,2},{4,3},{5,4},{6,5},{7,6},{8,7},{9,8},{10,9... | collective-permute-start | bytes 331784 | tf_op jit(solution)/shard_map/ppermute | solution.py:15
  223.0 4.1 %copy-start.22 = (pred[144,144]{0,1:T(8,128)(4,1)S(1)}, pred[144,144]{0,1:T(8,128)(4,1)}, u32[]{:S(2)}) copy-start(pred[144,144]{0,1:T(8,128)(4,1)} %broadcast_compare_fusion) | copy-start | bytes 62212
  232.5 3.2 %copy-start.19 = (pred[144,144]{0,1:T(8,128)(4,1)S(1)}, pred[144,144]{0,1:T(8,128)(4,1)}, u32[]{:S(2)}) copy-start(pred[144,144]{0,1:T(8,128)(4,1)} %broadcast_compare_fusion.1) | copy-start | bytes 62212
  243.2 8.4 %collective-permute-start.16 = (bf16[2,6,6,384]{3,2,1,0:T(8,128)(2,1)S(1)}, bf16[2,6,6,384]{3,2,1,0:T(8,128)(2,1)S(1)}, u32[]{:S(2)}, u32[]{:S(2)}) collective-permute-start(bf16[2,6,6,384]{3,2,1,0:T(8,128)(2,1)S(1)} %get-tuple-element.73), channel_id=1, source_target_pairs={{0,1},{1,2},{2,3},{3,4},{4,5},{5,6},{6,7},{7,8},{8,9},{9,10},{10,1... | collective-permute-start | bytes 165896 | tf_op jit(solution)/shard_map/ppermute | solution.py:15
  247.3 14.0 %copy-start.4 = (bf16[3,6,12,384]{3,2,1,0:T(8,128)(2,1)S(1)}, bf16[3,6,12,384]{3,2,1,0:T(8,128)(2,1)}, u32[]{:S(2)}) copy-start(bf16[3,6,12,384]{3,2,1,0:T(8,128)(2,1)} %copy-done.3) | copy-start | bytes 497668
  247.3 14.0 %copy-start.16 = (bf16[1,1,6,12,384]{4,3,2,1,0:T(8,128)(2,1)S(1)}, bf16[1,1,6,12,384]{4,3,2,1,0:T(8,128)(2,1)}, u32[]{:S(2)}) copy-start(bf16[1,1,6,12,384]{4,3,2,1,0:T(8,128)(2,1)} %get-tuple-element.67) | copy-start | bytes 165892
  247.4 8.4 %collective-permute-start.18 = (bf16[2,6,6,384]{3,2,1,0:T(8,128)(2,1)S(1)}, bf16[2,6,6,384]{3,2,1,0:T(8,128)(2,1)S(1)}, u32[]{:S(2)}, u32[]{:S(2)}) collective-permute-start(bf16[2,6,6,384]{3,2,1,0:T(8,128)(2,1)S(1)} %get-tuple-element.71), channel_id=1, source_target_pairs={{0,1},{1,2},{2,3},{3,4},{4,5},{5,6},{6,7},{7,8},{8,9},{9,10},{10,1... | collective-permute-start | bytes 165896 | tf_op jit(solution)/shard_map/ppermute | solution.py:15
  251.7 5.4 %collective-permute-start.17 = (bf16[2,3,12,384]{3,2,1,0:T(8,128)(2,1)S(1)}, bf16[2,3,12,384]{3,2,1,0:T(8,128)(2,1)S(1)}, u32[]{:S(2)}, u32[]{:S(2)}) collective-permute-start(bf16[2,3,12,384]{3,2,1,0:T(8,128)(2,1)S(1)} %fusion.422), channel_id=1, source_target_pairs={{0,32},{32,64},{64,96},{96,0},{1,33},{33,65},{65,97},{97,1},{2,34}... | collective-permute-start | bytes 165896 | tf_op jit(solution)/shard_map/ppermute | solution.py:15
  255.9 5.4 %collective-permute-start.19 = (bf16[2,3,12,384]{3,2,1,0:T(8,128)(2,1)S(1)}, bf16[2,3,12,384]{3,2,1,0:T(8,128)(2,1)S(1)}, u32[]{:S(2)}, u32[]{:S(2)}) collective-permute-start(bf16[2,3,12,384]{3,2,1,0:T(8,128)(2,1)S(1)} %fusion.421), channel_id=1, source_target_pairs={{0,32},{32,64},{64,96},{96,0},{1,33},{33,65},{65,97},{97,1},{2,34}... | collective-permute-start | bytes 165896 | tf_op jit(solution)/shard_map/ppermute | solution.py:15
  (12 other events, 19.0 us)
where the time goes:
time: 268 us; the launch traced here: 263 us
  local copies, waits for them, and re-layouts  106 us (40%)
  waiting for transfers between devices  66.7 us (25%)
  matrix products  50.5 us (19%)
  starting transfers between devices  21.2 us (8%)
  other arithmetic  17.1 us (6%)
    gather x3, local copies, waits for them, and re-layouts, body(): bias_grid = jnp.take(earth_bias[0], own_kinds, axis=0)[:, :, relative]  80.6 us
    ppermute x18, waiting for transfers between devices, from_behind(): return lax.ppermute(value, axis, pairs)  51.4 us
    dot_general x6, matrix products, window_core(): jnp.dot(activated, reduce_weight, preferred_element_type=jnp.float32)  23.5 us
    ppermute x18, starting transfers between devices, from_behind(): return lax.ppermute(value, axis, pairs)  18.6 us
    ppermute x2, waiting for transfers between devices, shifted(): return lax.ppermute(block, axis, route)  15.4 us
    dot_general x6, matrix products, window_core(): jnp.einsum('wqhd,wkhd->whqk', projected[:, :, 0], projected[:, :, 1], pre...  12 us
    convert_element_type x6, local copies, waits for them, and re-layouts, window_core(): jnp.dot(normed, joint_weight, preferred_element_type=jnp.float32)  9.38 us
    dot_general x6, matrix products, window_core(): jnp.einsum('whqk,wkhd->wqhd', attn_weights, projected[:, :, 2], preferred...  7.37 us
  transfers between devices with their start and end apart: 20, of which 17 were waited for; matrix products, arithmetic and copies ran while one was open for 40% of the time, Pallas kernels for 0%

commit v1 on v0

v1 whole, which is shorter than its diff:
```python
import functools

import jax
import jax.numpy as jnp
import numpy as np
from jax import lax
from jax.experimental import pallas as pl
from jax.experimental.pallas import tpu as pltpu
from jax.sharding import PartitionSpec as P

WIN_P = 2
WIN_H = 6
WIN_W = 12
TOK = WIN_P * WIN_H * WIN_W
LEVELS = 4
MICRO = 2
WIDTH = 384
HEADS = 12
FF = 1536
QROWS = 80
GRID_ROWS = LEVELS * WIN_H * 16
GROUP = 640
GUSED = 576
KDIM = 288
LOG2E = 1.4426950408889634
MESH = pl.DeviceIdType.MESH


def permutations():
    into = np.zeros((2, 2 * TOK, 4 * QROWS), np.float32)
    gather = np.zeros((4 * QROWS, GRID_ROWS), np.float32)
    plain = np.zeros((GRID_ROWS, 2 * TOK), np.float32)
    for level in range(LEVELS):
        for row in range(WIN_H):
            for col in range(WIN_W):
                token = (level // 2) * TOK + col * 12 + (level % 2) * 6 + row
                inner = (row % 3) * 6 + col % 6
                shifted_slot = (row >= 3) + 2 * (col >= 6)
                into[0, token, shifted_slot * QROWS + level * 18 + inner] = 1
                slot = (row < 3) + 2 * (col < 6)
                source = slot * QROWS + ((level + 3) % 4) * 18 + inner
                into[1, token, source] = 1
                place = (level * 6 + row) * 16 + col
                gather[source, place] = 1
                plain[place, token] = 1
    scatter = into[0].T.copy()
    back = gather.T.copy()
    return tuple(jnp.asarray(m, jnp.bfloat16) for m in (into, gather, scatter, back, plain))


def dot(a, b):
    return jnp.dot(a, b, preferred_element_type=jnp.float32)


def dot_nt(a, b):
    return lax.dot_general(a, b, (((1,), (1,)), ((), ())), preferred_element_type=jnp.float32)


def layer_norm(values, gain):
    average = jnp.mean(values, axis=-1, keepdims=True)
    centred = values - average
    spread = jnp.mean(centred * centred, axis=-1, keepdims=True)
    return centred * lax.rsqrt(spread + 1e-05) * gain


def gelu(x):
    return x * (0.5 + 0.5 * lax.erf(x * 0.7071067811865476))


def token_parts(token):
    col = (token * 5462) >> 16
    rest = token - col * 12
    level = (rest >= 6).astype(jnp.int32)
    return col, level, rest - level * 6


def lane_tokens():
    lane = lax.broadcasted_iota(jnp.int32, (1, 256), 1)
    return jnp.where(lane < 128, lane, 128 + (lane & 15))


def prepare_bias(first, lat, lon, lat_count, lon_count, class_ref, table_ref, rows_ref, bias_ref):
    rows_ref[...] = jnp.zeros_like(rows_ref)
    for i in range(2):
        for j in range(12):
            pb, rb = j // 6, j % 6
            for pa in range(2):
                begin = pb * 1656 + pa * 828 + rb * 138
                rows_ref[i, j, 0:12, pa * 144 : pa * 144 + 138] = table_ref[i, :, begin : begin + 138]
    to_row = lax.broadcasted_iota(jnp.int32, (192, 192), 0)
    to_col = lax.broadcasted_iota(jnp.int32, (192, 192), 1)
    swap = (((to_row & 15) << 4) + (to_row >> 4) == to_col).astype(jnp.float32).astype(jnp.bfloat16)
    by_head = [
        dot(swap, rows_ref[i].reshape(192, KDIM)).astype(jnp.bfloat16) for i in range(2)
    ]
    by_head = jnp.concatenate(by_head, axis=0)
    col_a, level_a, row_a = token_parts(lane_tokens())
    base = level_a * 144 + row_a * 23 + col_a + 11
    depth = lax.broadcasted_iota(jnp.int32, (KDIM, 256), 0)
    segment = lax.broadcasted_iota(jnp.int32, (12, 128), 1) >> 4
    for cb in range(12):
        pick = (depth == base - cb).astype(jnp.float32).astype(jnp.bfloat16)
        spread = dot(by_head, pick) * LOG2E
        for i in range(2):
            for g in range(3):
                tail = None
                for t in range(4):
                    start = i * 192 + (g * 4 + t) * 16
                    piece = spread[start : start + 12]
                    bias_ref[i, cb * 12 : cb * 12 + 12, g * GROUP + t * 128 : g * GROUP + t * 128 + 128] = piece[:, 0:128]
                    last = piece[:, 128:256]
                    tail = last if tail is None else jnp.where(segment == t, last, tail)
                bias_ref[i, cb * 12 : cb * 12 + 12, g * GROUP + 512 : g * GROUP + 640] = tail
    rows_all = 6 * lat_count
    cols_all = 12 * lon_count
    one = jnp.where(first, 1, 0)
    row_start = lat * 6 + 3 * one
    col_start = lon * 12 + 6 * one
    classes = class_ref[...].reshape(LEVELS * rows_all, cols_all).astype(jnp.float32).astype(jnp.bfloat16)
    col_b, level_b, row_b = token_parts(lax.broadcasted_iota(jnp.int32, (TOK, 1), 0))

    def wrap(v, extent):
        return jnp.where(v >= extent, v - extent, v)

    def onehot(a, b):
        return (a == b).astype(jnp.float32).astype(jnp.bfloat16)

    across = dot(
        classes,
        onehot(lax.broadcasted_iota(jnp.int32, (cols_all, 256), 0), wrap(col_start + col_a, cols_all)),
    )
    down = dot_nt(
        onehot(lax.broadcasted_iota(jnp.int32, (TOK, cols_all), 1), wrap(col_start + col_b, cols_all)),
        classes,
    )
    place_a = lax.broadcasted_iota(jnp.int32, across.shape, 0)
    place_b = lax.broadcasted_iota(jnp.int32, down.shape, 1)
    for i in range(2):

        def region(place, level, row, values, axis):
            at = ((2 * i + level + one) & 3) * rows_all + wrap(row_start + row, rows_all)
            value = jnp.sum(jnp.where(place == at, values, 0.0), axis=axis, keepdims=True)
            flags = 2 * (2 * i + level >= 3).astype(jnp.int32)
            flags = flags + (lat * 6 + row >= rows_all - 3).astype(jnp.int32)
            return 4.0 * value + (one * flags).astype(jnp.float32)

        region_a = region(place_a, level_a, row_a, across, 0)
        region_b = region(place_b, level_b, row_b, down, 1)
        same = region_b == region_a
        for g in range(3):
            for t in range(5):
                lanes = slice(g * GROUP + t * 128, g * GROUP + t * 128 + 128)
                part = same[:, 0:128] if t < 4 else same[:, 128:256]
                bias_ref[i, :, lanes] = jnp.where(part, bias_ref[i, :, lanes], -1e30)


def attention(query, key, value, bias_ref, i):
    head = lax.broadcasted_iota(jnp.int32, (1, 128), 1) >> 5
    keep = [(head == t).astype(jnp.float32).astype(jnp.bfloat16) for t in range(4)]
    ones = jnp.ones((16, TOK), jnp.bfloat16)
    mixed = []
    for g in range(3):
        lanes = slice(g * 128, g * 128 + 128)
        q, k, v = query[:, lanes], key[:, lanes], value[:, lanes]
        wide = jnp.concatenate([q[0:128] * m for m in keep] + [q[128:144] * m for m in keep], axis=0)
        scores = dot_nt(k, wide) + bias_ref[i, :, g * GROUP : g * GROUP + GUSED]
        top = jnp.max(scores, axis=0, keepdims=True)
        weights = jnp.exp2(scores - top).astype(jnp.bfloat16)
        v_turned = jnp.concatenate([jnp.transpose(v.astype(jnp.float32)).astype(jnp.bfloat16), ones], axis=0)
        out = dot(v_turned, weights)
        out = out[0:128] * (1.0 / out[128:129])
        main = jnp.concatenate(
            [out[t * 32 : t * 32 + 32, t * 128 : t * 128 + 128] for t in range(4)], axis=0
        )
        main = jnp.transpose(main).astype(jnp.bfloat16)
        tail = jnp.transpose(out[:, 512:576]).astype(jnp.bfloat16)
        tail = sum(tail[t * 16 : t * 16 + 16] * keep[t] for t in range(4))
        mixed.append(jnp.concatenate([main, tail], axis=0))
    return jnp.concatenate(mixed, axis=1)


def block(x, gains_ref, joint_ref, out_ref, expand_ref, reduce_ref, bias_ref):
    gains = gains_ref[...].astype(jnp.float32)
    normed = layer_norm(x, gains[0:1]).astype(jnp.bfloat16)
    projected = dot(normed, joint_ref[...])
    query = (projected[:, 0:WIDTH] * (LOG2E * 32**-0.5)).astype(jnp.bfloat16)
    key = projected[:, WIDTH : 2 * WIDTH].astype(jnp.bfloat16)
    value = projected[:, 2 * WIDTH :].astype(jnp.bfloat16)
    mixed = []
    for i in range(2):
        rows = slice(i * TOK, i * TOK + TOK)
        mixed.append(attention(query[rows], key[rows], value[rows], bias_ref, i))
    hidden = x + dot(jnp.concatenate(mixed, axis=0), out_ref[...])
    again = layer_norm(hidden, gains[1:2]).astype(jnp.bfloat16)
    total = hidden
    step = 512
    for start in range(0, FF, step):
        act = gelu(dot(again, expand_ref[:, start : start + step])).astype(jnp.bfloat16)
        total = total + dot(act, reduce_ref[start : start + step, :])
    return total.astype(jnp.bfloat16)


def kernel(
    lat_count,
    lon_count,
    fields_hbm,
    class_hbm,
    gains_hbm,
    joint_hbm,
    oproj_hbm,
    expand_hbm,
    reduce_hbm,
    table_hbm,
    into_hbm,
    gather_hbm,
    scatter_hbm,
    back_hbm,
    plain_hbm,
    result_ref,
    fields_ref,
    class_ref,
    gains_ref,
    joint_ref,
    oproj_ref,
    expand_ref,
    reduce_ref,
    table_ref,
    into_ref,
    gather_ref,
    scatter_ref,
    back_ref,
    plain_ref,
    grid_ref,
    rows_ref,
    bias_ref,
    halo_ref,
    take_ref,
    done_ref,
    home_ref,
    load_sem,
    halo_send,
    take_recv,
    home_send,
    home_recv,
    next_send,
):
    sec = lax.axis_index("section")
    lat = lax.axis_index("lat")
    lon = lax.axis_index("lon")
    first = sec == 0
    lat_up = lax.rem(lat + 1, lat_count)
    lat_down = lax.rem(lat + lat_count - 1, lat_count)
    lon_up = lax.rem(lon + 1, lon_count)
    lon_down = lax.rem(lon + lon_count - 1, lon_count)
    behind = [(lat, lon), (lat_down, lon), (lat, lon_down), (lat_down, lon_down)]
    ahead = [(lat, lon), (lat_up, lon), (lat, lon_up), (lat_up, lon_up)]

    barrier = pltpu.get_barrier_semaphore()

    @pl.when(first)
    def _():
        for where in behind[1:] + ahead[1:]:
            pl.semaphore_signal(barrier, inc=1, device_id=(0,) + where, device_id_type=MESH)

    @pl.when(jnp.logical_not(first))
    def _():
        for where in behind:
            pl.semaphore_signal(barrier, inc=1, device_id=(0,) + where, device_id_type=MESH)

    loads = []

    def load(src, dst):
        copy = pltpu.make_async_copy(src, dst, load_sem.at[len(loads)])
        copy.start()
        loads.append(copy)
        return copy

    load_fields = load(fields_hbm, fields_ref)
    load_gather = load(gather_hbm, gather_ref)
    prep = [load(table_hbm.at[0, i * lat_count + lat], table_ref.at[i]) for i in range(2)]
    prep.append(load(class_hbm, class_ref))
    rest = [
        load(into_hbm.at[sec], into_ref),
        load(gains_hbm.at[0], gains_ref),
        load(joint_hbm.at[0], joint_ref),
        load(oproj_hbm.at[0], oproj_ref),
        load(expand_hbm.at[0], expand_ref),
        load(reduce_hbm.at[0], reduce_ref),
        load(scatter_hbm, scatter_ref),
        load(back_hbm, back_ref),
        load(plain_hbm, plain_ref),
    ]

    def halo_copy(m, q):
        return pltpu.make_async_remote_copy(
            src_ref=halo_ref.at[m, q],
            dst_ref=take_ref.at[m, q],
            send_sem=halo_send.at[m, q],
            recv_sem=take_recv.at[m, q],
            device_id=(0,) + behind[q],
            device_id_type=MESH,
        )

    def home_copy(m, q):
        return pltpu.make_async_remote_copy(
            src_ref=done_ref.at[m, q],
            dst_ref=home_ref.at[m, q],
            send_sem=home_send.at[m, q],
            recv_sem=home_recv.at[m, q],
            device_id=(0,) + ahead[q],
            device_id_type=MESH,
        )

    def next_copy(m, q):
        return pltpu.make_async_remote_copy(
            src_ref=done_ref.at[m, q],
            dst_ref=take_ref.at[m, q],
            send_sem=next_send.at[m, q],
            recv_sem=take_recv.at[m, q],
            device_id=(1,) + ahead[q],
            device_id_type=MESH,
        )

    load_fields.wait()
    load_gather.wait()

    @pl.when(first)
    def _():
        grid_ref[...] = jnp.zeros_like(grid_ref)
        for m in range(MICRO):
            for p in range(LEVELS):
                for h in range(WIN_H):
                    grid_ref[m, p * 6 + h, 0:12, :] = fields_ref[m, p, h]
        for m in range(MICRO):
            sorted_rows = dot(gather_ref[...], grid_ref[m].reshape(GRID_ROWS, WIDTH)).astype(jnp.bfloat16)
            take_ref[m, 0] = sorted_rows[0:QROWS]
            for q in range(1, 4):
                halo_ref[m, q] = sorted_rows[q * QROWS : (q + 1) * QROWS]
            if m == 0:
                pl.semaphore_wait(barrier, 10)
            for q in (3, 2, 1):
                halo_copy(m, q).start()

    for copy in prep:
        copy.wait()
    prepare_bias(first, lat, lon, lat_count, lon_count, class_ref, table_ref, rows_ref, bias_ref)
    for copy in rest:
        copy.wait()

    def step(m, carry):
        @pl.when(first)
        def _():
            for q in range(1, 4):
                halo_copy(m, q).wait_recv()

        @pl.when(jnp.logical_not(first))
        def _():
            for q in range(4):
                next_copy(m, q).wait_recv()

        x = dot(into_ref[...], take_ref[m].reshape(4 * QROWS, WIDTH))
        y = block(x, gains_ref, joint_ref, oproj_ref, expand_ref, reduce_ref, bias_ref)

        @pl.when(first)
        def _():
            pieces = dot(scatter_ref[...], y).astype(jnp.bfloat16)
            done_ref[m] = pieces.reshape(4, QROWS, WIDTH)
            home_ref[m, 0] = pieces[0:QROWS]
            for q in (3, 2, 1, 0):
                next_copy(m, q).start()
            for q in (3, 2, 1):
                home_copy(m, q).start()

        @pl.when(jnp.logical_not(first))
        def _():
            write(m, dot(plain_ref[...], y).astype(jnp.bfloat16))

        return carry

    def write(m, rows):
        for p in range(LEVELS):
            for h in range(WIN_H):
                at = (p * 6 + h) * 16
                result_ref[m, p, h] = rows[at : at + 12]

    lax.fori_loop(0, MICRO, step, 0)

    @pl.when(first)
    def _():
        for m in range(MICRO):
            for q in range(1, 4):
                home_copy(m, q).wait_recv()
            write(m, dot(back_ref[...], home_ref[m].reshape(4 * QROWS, WIDTH)).astype(jnp.bfloat16))
        for m in range(MICRO):
            for q in range(1, 4):
                halo_copy(m, q).wait_send()
                home_copy(m, q).wait_send()
            for q in range(4):
                next_copy(m, q).wait_send()


def body(
    fields, surface_class, norm_gains, joint_proj, out_proj, expand_proj, reduce_proj, earth_bias
):
    lat_count = lax.axis_size("lat")
    lon_count = lax.axis_size("lon")
    matrices = permutations()
    operands = (
        fields, surface_class, norm_gains, joint_proj, out_proj, expand_proj, reduce_proj, earth_bias,
    ) + matrices
    bf16 = jnp.bfloat16
    scratch = [
        pltpu.VMEM(fields.shape, bf16),
        pltpu.VMEM(surface_class.shape, jnp.int32),
        pltpu.VMEM((2, WIDTH), bf16),
        pltpu.VMEM((WIDTH, 3 * WIDTH), bf16),
        pltpu.VMEM((WIDTH, WIDTH), bf16),
        pltpu.VMEM((WIDTH, FF), bf16),
        pltpu.VMEM((FF, WIDTH), bf16),
        pltpu.VMEM((2, HEADS, earth_bias.shape[-1]), bf16),
        pltpu.VMEM(matrices[0].shape[1:], bf16),
        pltpu.VMEM(matrices[1].shape, bf16),
        pltpu.VMEM(matrices[2].shape, bf16),
        pltpu.VMEM(matrices[3].shape, bf16),
        pltpu.VMEM(matrices[4].shape, bf16),
        pltpu.VMEM((MICRO, LEVELS * WIN_H, 16, WIDTH), bf16),
        pltpu.VMEM((2, 12, 16, KDIM), bf16),
        pltpu.VMEM((2, TOK, 3 * GROUP), jnp.float32),
        pltpu.VMEM((MICRO, 4, QROWS, WIDTH), bf16),
        pltpu.VMEM((MICRO, 4, QROWS, WIDTH), bf16),
        pltpu.VMEM((MICRO, 4, QROWS, WIDTH), bf16),
        pltpu.VMEM((MICRO, 4, QROWS, WIDTH), bf16),
        pltpu.SemaphoreType.DMA((14,)),
        pltpu.SemaphoreType.DMA((MICRO, 4)),
        pltpu.SemaphoreType.DMA((MICRO, 4)),
        pltpu.SemaphoreType.DMA((MICRO, 4)),
        pltpu.SemaphoreType.DMA((MICRO, 4)),
        pltpu.SemaphoreType.DMA((MICRO, 4)),
    ]
    result = pl.pallas_call(
        functools.partial(kernel, lat_count, lon_count),
        out_shape=jax.ShapeDtypeStruct(fields.shape, bf16),
        in_specs=[pl.BlockSpec(memory_space=pl.ANY)] * len(operands),
        out_specs=pl.BlockSpec(memory_space=pltpu.VMEM),
        scratch_shapes=scratch,
        compiler_params=pltpu.CompilerParams(
            collective_id=0, has_side_effects=True, vmem_limit_bytes=48 * 1024 * 1024
        ),
        name="two_blocks",
    )(*operands)
    return result[None]


def solution(mesh):
    return jax.shard_map(
        body,
        mesh=mesh,
        in_specs=(
            P(None, None, "lat", "lon", None),
            P(),
            P("section", None, None),
            P("section", None, None),
            P("section", None, None),
            P("section", None, None),
            P("section", None, None),
            P("section", None, None, None),
        ),
        out_specs=P("section", None, None, "lat", "lon", None),
        check_vma=False,
    )
```

time: 268 us -> 47.5 us (0.18); the launches traced: 263 us -> 47.3 us
  local copies, waits for them, and re-layouts: 106 us -> 9.13 us
  waiting for transfers between devices: 66.7 us -> 0 us
  matrix products: 50.5 us -> 0 us
  Pallas kernels: 0 us -> 38 us
  starting transfers between devices: 21.2 us -> 0 us
  other arithmetic: 17.1 us -> 0 us
    gather x3 -> x0, local copies, waits for them, and re-layouts: 80.6 us -> none  [body(): bias_grid = jnp.take(earth_bias[0], own_kinds, axis=0)[:, :, relative]]
    ppermute x20 -> x0, waiting for transfers between devices: 66.7 us -> none  [the longest x18 51.4 us: from_behind(): return lax.ppermute(value, axis, pairs)]
    dot_general x30 -> x0, matrix products: 50.5 us -> none  [the longest x6 23.5 us: window_core(): jnp.dot(activated, reduce_weight, preferred_element_type=jnp.float32)]
    pallas_call x0 -> x1, Pallas kernels: none -> 38 us  [body(): pl.pallas_call(functools.partial(kernel, lat_count, lon_count), out_shape...]
    ppermute x20 -> x0, starting transfers between devices: 21.2 us -> none  [the longest x18 18.6 us: from_behind(): return lax.ppermute(value, axis, pairs)]
    convert_element_type x18 -> x0, local copies, waits for them, and re-layouts: 16.2 us -> none  [the longest x6 9.38 us: window_core(): jnp.dot(normed, joint_weight, preferred_element_type=jnp.float32)]
    unnamed x49 -> x22, local copies, waits for them, and re-layouts: 1.35 us -> 8.14 us
    reduce_sum x21 -> x0, other arithmetic: 5.01 us -> none  [the longest x9 1.92 us: layer_norm(): spread = jnp.mean(centred * centred, axis=-1, keepdims=True)]
  transfers between devices with their start and end apart: 20 -> 0, of which waited for: 17 -> 0; matrix products, arithmetic and copies ran while one was open for 40% -> 0% of each run, Pallas kernels for 0% -> 0%
where the time goes in v1:
time: 47.5 us; the launch traced here: 47.3 us
  Pallas kernels  38 us (80%)
  local copies, waits for them, and re-layouts  9.13 us (19%)
    pallas_call x1, Pallas kernels, body(): pl.pallas_call(functools.partial(kernel, lat_count, lon_count), out_shape...  38 us
    unnamed x22, local copies, waits for them, and re-layouts  8.14 us
    broadcast_in_dim x1, local copies, waits for them, and re-layouts, body(): return result[None]  0.99 us

profile of v1, /device:TPU:2, one launch (start us, length us, event | category | flops | bytes accessed | tf_op | source)
XLA Modules:
  0.0 47.3 jit_solution(11803897515568725138)
XLA Ops:
  0.0 0.0 copy-start.2
  0.0 0.0 copy-start
  0.0 0.0 copy-start.1
  0.0 0.0 copy-start.9
  0.0 1.2 %copy.14.fields_hbm = bf16[2,4,6,12,384]{4,3,2,1,0:T(8,128)(2,1)S(1)} copy(bf16[2,4,6,12,384]{4,1,3,2,0:T(4,128)(2,1)} %param.13) | data formatting | bytes 884736 | tf_op args[0]
  1.3 1.2 %copy.15.table_hbm = bf16[1,8,12,3312]{3,2,1,0:T(8,128)(2,1)S(1)} copy(bf16[1,8,12,3312]{3,1,2,0:T(8,128)(2,1)} %param.20) | data formatting | bytes 1271808 | tf_op args[7]
  2.5 0.0 copy-done.2
  2.5 0.0 copy-done
  2.5 0.0 copy-done.1
  2.5 0.0 copy-done.9
  2.5 0.0 copy-start.3
  2.5 1.0 %copy-done.3 = bf16[1,384,384]{2,1,0:T(8,128)(2,1)S(1)} copy-done((bf16[1,384,384]{2,1,0:T(8,128)(2,1)S(1)}, bf16[1,384,384]{2,1,0:T(8,128)(2,1)}, u32[]{:S(2)}) %copy-start.3) | copy-done | bytes 294936
  3.5 0.0 copy-start.4
  3.5 1.0 %copy-done.4 = bf16[384,288]{1,0:T(8,128)(2,1)S(1)} copy-done((bf16[384,288]{1,0:T(8,128)(2,1)S(1)}, bf16[384,288]{1,0:T(8,128)(2,1)}, u32[]{:S(2)}) %copy-start.4) | copy-done | bytes 221208
  4.4 0.0 copy-start.5
  4.4 1.0 %copy-done.5 = bf16[384,320]{1,0:T(8,128)(2,1)S(1)} copy-done((bf16[384,320]{1,0:T(8,128)(2,1)S(1)}, bf16[384,320]{1,0:T(8,128)(2,1)}, u32[]{:S(2)}) %copy-start.5) | copy-done | bytes 245784
  5.4 0.0 copy-start.6
  5.4 0.9 %copy-done.6 = bf16[320,288]{1,0:T(8,128)(2,1)S(1)} copy-done((bf16[320,288]{1,0:T(8,128)(2,1)S(1)}, bf16[320,288]{1,0:T(8,128)(2,1)}, u32[]{:S(2)}) %copy-start.6) | copy-done | bytes 184344
  6.3 0.0 copy-start.7
  6.3 0.9 %copy-done.7 = bf16[320,384]{1,0:T(8,128)(2,1)S(1)} copy-done((bf16[320,384]{1,0:T(8,128)(2,1)S(1)}, bf16[320,384]{1,0:T(8,128)(2,1)}, u32[]{:S(2)}) %copy-start.7) | copy-done | bytes 245784
  7.3 0.0 copy-start.8
  7.3 0.9 %copy-done.8 = s32[4,24,384]{2,1,0:T(8,128)S(1)} copy-done((s32[4,24,384]{2,1,0:T(8,128)S(1)}, s32[4,24,384]{2,1,0:T(8,128)}, u32[]{:S(2)}) %copy-start.8) | copy-done | bytes 147480
  8.2 38.0 %two_blocks.1 = bf16[2,4,6,12,384]{4,3,2,1,0:T(8,128)(2,1)S(1)} custom-call(bf16[2,4,6,12,384]{4,3,2,1,0:T(8,128)(2,1)S(1)} %copy.14.fields_hbm, s32[4,24,384]{2,1,0:T(8,128)S(1)} %copy-done.8, bf16[1,2,384]{2,1,0:T(2,128)(2,1)S(1)} %copy-done.9, bf16[1,384,1152]{2,1,0:T(8,128)(2,1)S(1)} %copy-done.1, bf16[1,384,384]{2,1,0:T(8,128)(2,1)S(1)} %copy-done.3, ...), custom_call_target="tpu_custom_call" | custom-call | tf_op jit(solution)/shard_map/two_blocks/pallas_call | solution.py:440
  46.3 1.0 %copy.16 = bf16[1,2,4,6,12,384]{5,2,4,3,1,0:T(4,128)(2,1)} copy(bf16[1,2,4,6,12,384]{5,4,3,2,1,0:T(8,128)(2,1)S(1)} %bitcast.1) | data formatting | bytes 884736 | tf_op jit(solution)/shard_map/broadcast_in_dim | solution.py:451
Async XLA Ops:
  0.0 2.5 %copy-start.2 = (bf16[2,288,320]{2,1,0:T(8,128)(2,1)S(1)}, bf16[2,288,320]{2,1,0:T(8,128)(2,1)}, u32[]{:S(2)}) copy-start(bf16[2,288,320]{2,1,0:T(8,128)(2,1)} %constant.10.clone.into_hbm) | copy-start | bytes 1105924
  0.0 2.5 %copy-start = (bf16[1,384,1536]{2,1,0:T(8,128)(2,1)S(1)}, bf16[1,384,1536]{2,1,0:T(8,128)(2,1)}, u32[]{:S(2)}) copy-start(bf16[1,384,1536]{2,1,0:T(8,128)(2,1)} %expand_hbm.1) | copy-start | bytes 3538948
  0.0 2.5 %copy-start.1 = (bf16[1,384,1152]{2,1,0:T(8,128)(2,1)S(1)}, bf16[1,384,1152]{2,1,0:T(8,128)(2,1)}, u32[]{:S(2)}) copy-start(bf16[1,384,1152]{2,1,0:T(8,128)(2,1)} %joint_hbm.1) | copy-start | bytes 2654212
  0.0 2.5 %copy-start.9 = (bf16[1,2,384]{2,1,0:T(2,128)(2,1)S(1)}, bf16[1,2,384]{2,1,0:T(2,128)(2,1)}, u32[]{:S(2)}) copy-start(bf16[1,2,384]{2,1,0:T(2,128)(2,1)} %gains_hbm.1) | copy-start | bytes 4612
  2.5 1.0 %copy-start.3 = (bf16[1,384,384]{2,1,0:T(8,128)(2,1)S(1)}, bf16[1,384,384]{2,1,0:T(8,128)(2,1)}, u32[]{:S(2)}) copy-start(bf16[1,384,384]{2,1,0:T(8,128)(2,1)} %oproj_hbm.1) | copy-start | bytes 884740
  3.5 1.0 %copy-start.4 = (bf16[384,288]{1,0:T(8,128)(2,1)S(1)}, bf16[384,288]{1,0:T(8,128)(2,1)}, u32[]{:S(2)}) copy-start(bf16[384,288]{1,0:T(8,128)(2,1)} %constant.14.clone.plain_hbm) | copy-start | bytes 663556
  4.4 1.0 %copy-start.5 = (bf16[384,320]{1,0:T(8,128)(2,1)S(1)}, bf16[384,320]{1,0:T(8,128)(2,1)}, u32[]{:S(2)}) copy-start(bf16[384,320]{1,0:T(8,128)(2,1)} %constant.13.clone.back_hbm) | copy-start | bytes 737284
  5.4 0.9 %copy-start.6 = (bf16[320,288]{1,0:T(8,128)(2,1)S(1)}, bf16[320,288]{1,0:T(8,128)(2,1)}, u32[]{:S(2)}) copy-start(bf16[320,288]{1,0:T(8,128)(2,1)} %constant.12.clone.scatter_hbm) | copy-start | bytes 552964
  6.3 0.9 %copy-start.7 = (bf16[320,384]{1,0:T(8,128)(2,1)S(1)}, bf16[320,384]{1,0:T(8,128)(2,1)}, u32[]{:S(2)}) copy-start(bf16[320,384]{1,0:T(8,128)(2,1)} %constant.11.clone.gather_hbm) | copy-start | bytes 737284
  7.3 0.9 %copy-start.8 = (s32[4,24,384]{2,1,0:T(8,128)S(1)}, s32[4,24,384]{2,1,0:T(8,128)}, u32[]{:S(2)}) copy-start(s32[4,24,384]{2,1,0:T(8,128)} %class_hbm.1) | copy-start | bytes 442372

commit v2 on v1

--- a/solution.py
+++ b/solution.py
@@ -2,7 +2,6 @@
 
 import jax
 import jax.numpy as jnp
-import numpy as np
 from jax import lax
 from jax.experimental import pallas as pl
 from jax.experimental.pallas import tpu as pltpu
@@ -18,7 +17,7 @@
 HEADS = 12
 FF = 1536
 QROWS = 80
-GRID_ROWS = LEVELS * WIN_H * 16
+GRID_ROWS = LEVELS * WIN_H * WIN_W
 GROUP = 640
 GUSED = 576
 KDIM = 288
@@ -26,26 +25,84 @@
 MESH = pl.DeviceIdType.MESH
 
 
-def permutations():
-    into = np.zeros((2, 2 * TOK, 4 * QROWS), np.float32)
-    gather = np.zeros((4 * QROWS, GRID_ROWS), np.float32)
-    plain = np.zeros((GRID_ROWS, 2 * TOK), np.float32)
-    for level in range(LEVELS):
-        for row in range(WIN_H):
-            for col in range(WIN_W):
-                token = (level // 2) * TOK + col * 12 + (level % 2) * 6 + row
-                inner = (row % 3) * 6 + col % 6
-                shifted_slot = (row >= 3) + 2 * (col >= 6)
-                into[0, token, shifted_slot * QROWS + level * 18 + inner] = 1
-                slot = (row < 3) + 2 * (col < 6)
-                source = slot * QROWS + ((level + 3) % 4) * 18 + inner
-                into[1, token, source] = 1
-                place = (level * 6 + row) * 16 + col
-                gather[source, place] = 1
-                plain[place, token] = 1
-    scatter = into[0].T.copy()
-    back = gather.T.copy()
-    return tuple(jnp.asarray(m, jnp.bfloat16) for m in (into, gather, scatter, back, plain))
+def divide(value, by):
+    return (value * (-(-65536 // by))) >> 16
+
+
+def token_parts(token):
+    col = divide(token, 12)
+    rest = token - col * 12
+    level = (rest >= 6).astype(jnp.int32)
+    return col, level, rest - level * 6
+
+
+def slot_row(row_half, col_half, level, row, col):
+    return (row_half + 2 * col_half) * QROWS + level * 18 + row * 6 + col
+
+
+def halves(position, extent):
+    half = (position >= extent).astype(jnp.int32)
+    return half, position - half * extent
+
+
+def one_hot(rows, target):
+    at = lax.broadcasted_iota(jnp.int32, (rows, target.shape[1]), 0)
+    return (at == target).astype(jnp.float32).astype(jnp.bfloat16)
+
+
+def grid_place(row, col, level):
+    return (row * 12 + col) * 4 + level
+
+
+def gather_matrix():
+    place = lax.broadcasted_iota(jnp.int32, (1, GRID_ROWS), 1)
+    pair = place >> 2
+    row = divide(pair, 12)
+    row_half, row_in = halves(row, 3)
+    col_half, col_in = halves(pair - row * 12, 6)
+    level = ((place & 3) + 3) & 3
+    return one_hot(4 * QROWS, slot_row(1 - row_half, 1 - col_half, level, row_in, col_in))
+
+
+def scatter_matrix():
+    token = lax.broadcasted_iota(jnp.int32, (1, 2 * TOK), 1)
+    window, rest = halves(token, TOK)
+    col, level, row = token_parts(rest)
+    row_half, row_in = halves(row, 3)
+    col_half, col_in = halves(col, 6)
+    return one_hot(4 * QROWS, slot_row(row_half, col_half, 2 * window + level, row_in, col_in))
+
+
+def slot_parts():
+    place = lax.broadcasted_iota(jnp.int32, (1, 4 * QROWS), 1)
+    slot = divide(place, QROWS)
+    rest = place - slot * QROWS
+    level = divide(rest, 18)
+    inner = rest - level * 18
+    row = divide(inner, 6)
+    return rest < 72, slot & 1, slot >> 1, level, row, inner - row * 6
+
+
+def into_matrix(one):
+    used, row_half, col_half, level, row, col = slot_parts()
+    row = row + 3 * (row_half * one + (1 - row_half) * (1 - one))
+    col = col + 6 * (col_half * one + (1 - col_half) * (1 - one))
+    level = (level + 1 - one) & 3
+    token = (level >> 1) * TOK + col * 12 + (level & 1) * 6 + row
+    return one_hot(2 * TOK, jnp.where(used, token, -1))
+
+
+def back_matrix():
+    used, row_half, col_half, level, row, col = slot_parts()
+    place = grid_place(row + 3 * (1 - row_half), col + 6 * (1 - col_half), (level + 1) & 3)
+    return one_hot(GRID_ROWS, jnp.where(used, place, -1))
+
+
+def plain_matrix():
+    token = lax.broadcasted_iota(jnp.int32, (1, 2 * TOK), 1)
+    window, rest = halves(token, TOK)
+    col, level, row = token_parts(rest)
+    return one_hot(GRID_ROWS, grid_place(row, col, 2 * window + level))
 
 
 def dot(a, b):
@@ -67,26 +124,27 @@
     return x * (0.5 + 0.5 * lax.erf(x * 0.7071067811865476))
 
 
-def token_parts(token):
-    col = (token * 5462) >> 16
-    rest = token - col * 12
-    level = (rest >= 6).astype(jnp.int32)
-    return col, level, rest - level * 6
-
-
 def lane_tokens():
     lane = lax.broadcasted_iota(jnp.int32, (1, 256), 1)
     return jnp.where(lane < 128, lane, 128 + (lane & 15))
 
 
 def prepare_bias(first, lat, lon, lat_count, lon_count, class_ref, table_ref, rows_ref, bias_ref):
+    kinds = 2 * lat_count
+    to_row = lax.broadcasted_iota(jnp.int32, (32, HEADS * kinds), 0)
+    to_col = lax.broadcasted_iota(jnp.int32, (32, HEADS * kinds), 1)
+    wanted = (to_row & 15) * kinds + (to_row >> 4) * lat_count + lat
+    own = (to_col == wanted).astype(jnp.float32).astype(jnp.bfloat16)
+    table = dot(own, table_ref[...].reshape(HEADS * kinds, -1)).astype(jnp.bfloat16)
     rows_ref[...] = jnp.zeros_like(rows_ref)
     for i in range(2):
         for j in range(12):
             pb, rb = j // 6, j % 6
             for pa in range(2):
                 begin = pb * 1656 + pa * 828 + rb * 138
-                rows_ref[i, j, 0:12, pa * 144 : pa * 144 + 138] = table_ref[i, :, begin : begin + 138]
+                rows_ref[i, j, :, pa * 144 : pa * 144 + 138] = table[
+                    i * 16 : i * 16 + 16, begin : begin + 138
+                ]
     to_row = lax.broadcasted_iota(jnp.int32, (192, 192), 0)
     to_col = lax.broadcasted_iota(jnp.int32, (192, 192), 1)
     swap = (((to_row & 15) << 4) + (to_row >> 4) == to_col).astype(jnp.float32).astype(jnp.bfloat16)
@@ -211,11 +269,6 @@
     expand_hbm,
     reduce_hbm,
     table_hbm,
-    into_hbm,
-    gather_hbm,
-    scatter_hbm,
-    back_hbm,
-    plain_hbm,
     result_ref,
     fields_ref,
     class_ref,
@@ -226,11 +279,8 @@
     reduce_ref,
     table_ref,
     into_ref,
-    gather_ref,
     scatter_ref,
-    back_ref,
-    plain_ref,
-    grid_ref,
+    last_ref,
     rows_ref,
     bias_ref,
     halo_ref,
@@ -276,19 +326,13 @@
         return copy
 
     load_fields = load(fields_hbm, fields_ref)
-    load_gather = load(gather_hbm, gather_ref)
-    prep = [load(table_hbm.at[0, i * lat_count + lat], table_ref.at[i]) for i in range(2)]
-    prep.append(load(class_hbm, class_ref))
+    prep = [load(table_hbm.at[0], table_ref), load(class_hbm, class_ref)]
     rest = [
-        load(into_hbm.at[sec], into_ref),
         load(gains_hbm.at[0], gains_ref),
         load(joint_hbm.at[0], joint_ref),
         load(oproj_hbm.at[0], oproj_ref),
         load(expand_hbm.at[0], expand_ref),
         load(reduce_hbm.at[0], reduce_ref),
-        load(scatter_hbm, scatter_ref),
-        load(back_hbm, back_ref),
-        load(plain_hbm, plain_ref),
     ]
 
     def halo_copy(m, q):
@@ -322,17 +366,12 @@
         )
 
     load_fields.wait()
-    load_gather.wait()
 
     @pl.when(first)
     def _():
-        grid_ref[...] = jnp.zeros_like(grid_ref)
+        gather = gather_matrix()
         for m in range(MICRO):
-            for p in range(LEVELS):
-                for h in range(WIN_H):
-                    grid_ref[m, p * 6 + h, 0:12, :] = fields_ref[m, p, h]
-        for m in range(MICRO):
-            sorted_rows = dot(gather_ref[...], grid_ref[m].reshape(GRID_ROWS, WIDTH)).astype(jnp.bfloat16)
+            sorted_rows = dot(gather, fields_ref[m].reshape(GRID_ROWS, WIDTH)).astype(jnp.bfloat16)
             take_ref[m, 0] = sorted_rows[0:QROWS]
             for q in range(1, 4):
                 halo_ref[m, q] = sorted_rows[q * QROWS : (q + 1) * QROWS]
@@ -340,6 +379,17 @@
                 pl.semaphore_wait(barrier, 10)
             for q in (3, 2, 1):
                 halo_copy(m, q).start()
+
+    into_ref[...] = into_matrix(jnp.where(first, 1, 0))
+
+    @pl.when(first)
+    def _():
+        scatter_ref[...] = scatter_matrix()
+        last_ref[...] = back_matrix()
+
+    @pl.when(jnp.logical_not(first))
+    def _():
+        last_ref[:, 0 : 2 * TOK] = plain_matrix()
 
     for copy in prep:
         copy.wait()
@@ -373,15 +423,12 @@
 
         @pl.when(jnp.logical_not(first))
         def _():
-            write(m, dot(plain_ref[...], y).astype(jnp.bfloat16))
+            write(m, dot(last_ref[:, 0 : 2 * TOK], y).astype(jnp.bfloat16))
 
         return carry
 
     def write(m, rows):
-        for p in range(LEVELS):
-            for h in range(WIN_H):
-                at = (p * 6 + h) * 16
-                result_ref[m, p, h] = rows[at : at + 12]
+        result_ref[m] = rows.reshape(WIN_H, WIN_W, LEVELS, WIDTH)
 
     lax.fori_loop(0, MICRO, step, 0)
 
@@ -390,7 +437,7 @@
         for m in range(MICRO):
             for q in range(1, 4):
                 home_copy(m, q).wait_recv()
-            write(m, dot(back_ref[...], home_ref[m].reshape(4 * QROWS, WIDTH)).astype(jnp.bfloat16))
+            write(m, dot(last_ref[...], home_ref[m].reshape(4 * QROWS, WIDTH)).astype(jnp.bfloat16))
         for m in range(MICRO):
             for q in range(1, 4):
                 halo_copy(m, q).wait_send()
@@ -404,10 +451,11 @@
 ):
     lat_count = lax.axis_size("lat")
     lon_count = lax.axis_size("lon")
-    matrices = permutations()
+    fields = jnp.transpose(fields, (0, 2, 3, 1, 4))
     operands = (
-        fields, surface_class, norm_gains, joint_proj, out_proj, expand_proj, reduce_proj, earth_bias,
-    ) + matrices
+        fields, surface_class, norm_gains, joint_proj, out_proj, expand_proj, reduce_proj,
+        jnp.transpose(earth_bias, (0, 2, 1, 3)),
+    )
     bf16 = jnp.bfloat16
     scratch = [
         pltpu.VMEM(fields.shape, bf16),
@@ -417,13 +465,10 @@
         pltpu.VMEM((WIDTH, WIDTH), bf16),
         pltpu.VMEM((WIDTH, FF), bf16),
         pltpu.VMEM((FF, WIDTH), bf16),
-        pltpu.VMEM((2, HEADS, earth_bias.shape[-1]), bf16),
-        pltpu.VMEM(matrices[0].shape[1:], bf16),
-        pltpu.VMEM(matrices[1].shape, bf16),
-        pltpu.VMEM(matrices[2].shape, bf16),
-        pltpu.VMEM(matrices[3].shape, bf16),
-        pltpu.VMEM(matrices[4].shape, bf16),
-        pltpu.VMEM((MICRO, LEVELS * WIN_H, 16, WIDTH), bf16),
+        pltpu.VMEM((HEADS,) + earth_bias.shape[1:2] + earth_bias.shape[3:], bf16),
+        pltpu.VMEM((2 * TOK, 4 * QROWS), bf16),
+        pltpu.VMEM((4 * QROWS, 2 * TOK), bf16),
+        pltpu.VMEM((GRID_ROWS, 4 * QROWS), bf16),
         pltpu.VMEM((2, 12, 16, KDIM), bf16),
         pltpu.VMEM((2, TOK, 3 * GROUP), jnp.float32),
         pltpu.VMEM((MICRO, 4, QROWS, WIDTH), bf16),
@@ -444,11 +489,11 @@
         out_specs=pl.BlockSpec(memory_space=pltpu.VMEM),
         scratch_shapes=scratch,
         compiler_params=pltpu.CompilerParams(
-            collective_id=0, has_side_effects=True, vmem_limit_bytes=48 * 1024 * 1024
+            collective_id=0, has_side_effects=True, vmem_limit_bytes=63 * 1024 * 1024
         ),
         name="two_blocks",
     )(*operands)
-    return result[None]
+    return jnp.transpose(result, (0, 3, 1, 2, 4))[None]
 
 
 def solution(mesh):

time: 47.5 us -> 40.8 us (0.86)
  local copies, waits for them, and re-layouts: 9.13 us -> 1.93 us
  Pallas kernels: 38 us -> 38.8 us
    unnamed x22 -> x1, local copies, waits for them, and re-layouts: 8.14 us -> 1.93 us
    broadcast_in_dim x1 -> x0, local copies, waits for them, and re-layouts: 0.99 us -> none  [body(): return result[None]]
    pallas_call x1, Pallas kernels: 38 us -> 38.8 us  [body(): pl.pallas_call(functools.partial(kernel, lat_count, lon_count), out_shape...]
where the time goes in v2:
time: 40.8 us; the launch traced here: 40.7 us
  Pallas kernels  38.8 us (95%)
  local copies, waits for them, and re-layouts  1.93 us (5%)
    pallas_call x1, Pallas kernels, body(): pl.pallas_call(functools.partial(kernel, lat_count, lon_count), out_shape...  38.8 us
    unnamed x1, local copies, waits for them, and re-layouts  1.93 us

profile of v2, /device:TPU:2, one launch (start us, length us, event | category | flops | bytes accessed | tf_op | source)
XLA Modules:
  0.0 40.7 jit_solution(14259779134830186880)
XLA Ops:
  0.0 38.8 %two_blocks.1 = bf16[2,6,12,4,384]{4,3,2,1,0:T(4,128)(2,1)} custom-call(bf16[2,6,12,4,384]{4,3,2,1,0:T(4,128)(2,1)} %bitcast.7, s32[4,24,384]{2,1,0:T(8,128)} %class_hbm.1, bf16[1,2,384]{2,1,0:T(2,128)(2,1)} %gains_hbm.1, bf16[1,384,1152]{2,1,0:T(8,128)(2,1)} %joint_hbm.1, bf16[1,384,384]{2,1,0:T(8,128)(2,1)} %oproj_hbm.1, bf16[1,384,1536]{2,1,0:T(8,128)(2,1)} %expand_hbm.1, ...), custom_call_target="tpu_custom_call" | custom-call | tf_op jit(solution)/shard_map/two_blocks/pallas_call | solution.py:485
  38.8 1.9 %copy.10 = bf16[1,2,4,6,12,384]{5,2,4,3,1,0:T(4,128)(2,1)} copy(bf16[1,2,4,6,12,384]{5,2,4,3,1,0:T(4,128)(2,1)} %bitcast.5) | data formatting | bytes 884736

commit v3 on v2

--- a/solution.py
+++ b/solution.py
@@ -129,7 +129,7 @@
     return jnp.where(lane < 128, lane, 128 + (lane & 15))
 
 
-def prepare_bias(first, lat, lon, lat_count, lon_count, class_ref, table_ref, rows_ref, bias_ref):
+def prepare_bias(first, lat, lon, lat_count, lon_count, class_ref, table_ref, rows_ref, turned_ref, bias_ref):
     kinds = 2 * lat_count
     to_row = lax.broadcasted_iota(jnp.int32, (32, HEADS * kinds), 0)
     to_col = lax.broadcasted_iota(jnp.int32, (32, HEADS * kinds), 1)
@@ -155,20 +155,13 @@
     col_a, level_a, row_a = token_parts(lane_tokens())
     base = level_a * 144 + row_a * 23 + col_a + 11
     depth = lax.broadcasted_iota(jnp.int32, (KDIM, 256), 0)
-    segment = lax.broadcasted_iota(jnp.int32, (12, 128), 1) >> 4
     for cb in range(12):
         pick = (depth == base - cb).astype(jnp.float32).astype(jnp.bfloat16)
-        spread = dot(by_head, pick) * LOG2E
+        spread = dot(by_head, pick)
         for i in range(2):
-            for g in range(3):
-                tail = None
-                for t in range(4):
-                    start = i * 192 + (g * 4 + t) * 16
-                    piece = spread[start : start + 12]
-                    bias_ref[i, cb * 12 : cb * 12 + 12, g * GROUP + t * 128 : g * GROUP + t * 128 + 128] = piece[:, 0:128]
-                    last = piece[:, 128:256]
-                    tail = last if tail is None else jnp.where(segment == t, last, tail)
-                bias_ref[i, cb * 12 : cb * 12 + 12, g * GROUP + 512 : g * GROUP + 640] = tail
+            for h in range(HEADS):
+                start = i * 192 + h * 16
+                turned_ref[i * HEADS + h, cb * 12 : cb * 12 + 12, :] = spread[start : start + 12]
     rows_all = 6 * lat_count
     cols_all = 12 * lon_count
     one = jnp.where(first, 1, 0)
@@ -191,6 +184,10 @@
         onehot(lax.broadcasted_iota(jnp.int32, (TOK, cols_all), 1), wrap(col_start + col_b, cols_all)),
         classes,
     )
+    identity = (
+        lax.broadcasted_iota(jnp.int32, (TOK, 256), 0) == lax.broadcasted_iota(jnp.int32, (TOK, 256), 1)
+    )
+    identity = identity.astype(jnp.float32).astype(jnp.bfloat16)
     place_a = lax.broadcasted_iota(jnp.int32, across.shape, 0)
     place_b = lax.broadcasted_iota(jnp.int32, down.shape, 1)
     for i in range(2):
@@ -206,34 +203,43 @@
         region_b = region(place_b, level_b, row_b, down, 1)
         same = region_b == region_a
         for g in range(3):
+            heads = [turned_ref[i * HEADS + g * 4 + t] for t in range(4)]
+            stack = jnp.concatenate([h[0:128] for h in heads] + [h[128:144] for h in heads], axis=0)
+            spread = dot_nt(identity, stack.astype(jnp.bfloat16)) * LOG2E
             for t in range(5):
-                lanes = slice(g * GROUP + t * 128, g * GROUP + t * 128 + 128)
-                part = same[:, 0:128] if t < 4 else same[:, 128:256]
-                bias_ref[i, :, lanes] = jnp.where(part, bias_ref[i, :, lanes], -1e30)
+                lanes = slice(t * 128, min(t * 128 + 128, GUSED))
+                part = same[:, 0:128] if t < 4 else same[:, 128:192]
+                to = slice(g * GROUP + lanes.start, g * GROUP + lanes.stop)
+                bias_ref[i, :, to] = jnp.where(part, spread[:, lanes], -1e30)
+            bias_ref[i, :, g * GROUP + GUSED : (g + 1) * GROUP] = jnp.full((TOK, GROUP - GUSED), -1e30, jnp.float32)
 
 
 def attention(query, key, value, bias_ref, i):
     head = lax.broadcasted_iota(jnp.int32, (1, 128), 1) >> 5
     keep = [(head == t).astype(jnp.float32).astype(jnp.bfloat16) for t in range(4)]
-    ones = jnp.ones((16, TOK), jnp.bfloat16)
+    segment = lax.broadcasted_iota(jnp.int32, (1, 128), 1) >> 4
+    blank = jnp.zeros((64, 128), jnp.bfloat16)
+    blank_wide = jnp.zeros((64, 256), jnp.bfloat16)
     mixed = []
     for g in range(3):
         lanes = slice(g * 128, g * 128 + 128)
         q, k, v = query[:, lanes], key[:, lanes], value[:, lanes]
-        wide = jnp.concatenate([q[0:128] * m for m in keep] + [q[128:144] * m for m in keep], axis=0)
-        scores = dot_nt(k, wide) + bias_ref[i, :, g * GROUP : g * GROUP + GUSED]
-        top = jnp.max(scores, axis=0, keepdims=True)
-        weights = jnp.exp2(scores - top).astype(jnp.bfloat16)
-        v_turned = jnp.concatenate([jnp.transpose(v.astype(jnp.float32)).astype(jnp.bfloat16), ones], axis=0)
-        out = dot(v_turned, weights)
-        out = out[0:128] * (1.0 / out[128:129])
-        main = jnp.concatenate(
-            [out[t * 32 : t * 32 + 32, t * 128 : t * 128 + 128] for t in range(4)], axis=0
-        )
-        main = jnp.transpose(main).astype(jnp.bfloat16)
-        tail = jnp.transpose(out[:, 512:576]).astype(jnp.bfloat16)
-        tail = sum(tail[t * 16 : t * 16 + 16] * keep[t] for t in range(4))
-        mixed.append(jnp.concatenate([main, tail], axis=0))
+        wide = jnp.concatenate([k[0:128] * m for m in keep] + [k[128:144] * m for m in keep] + [blank], axis=0)
+        scores = dot_nt(q, wide) + bias_ref[i, :, g * GROUP : (g + 1) * GROUP]
+        tail = scores[:, 512:640]
+        top, weights = [], []
+        for t in range(4):
+            main = scores[:, t * 128 : t * 128 + 128]
+            joined = jnp.maximum(main, jnp.where(segment == t, tail, -1e30))
+            top.append(jnp.max(joined, axis=1, keepdims=True))
+            weights.append(jnp.exp2(main - top[t]).astype(jnp.bfloat16))
+        tops = jnp.where(segment < 2, jnp.where(segment == 0, top[0], top[1]), jnp.where(segment == 2, top[2], top[3]))
+        weights.append(jnp.exp2(tail - tops).astype(jnp.bfloat16))
+        weights = jnp.concatenate(weights, axis=1)
+        pairs = [jnp.concatenate([v[0:128] * m, jnp.broadcast_to(m, (128, 128))], axis=1) for m in keep]
+        pairs += [jnp.concatenate([v[128:144] * m, jnp.broadcast_to(m, (16, 128))], axis=1) for m in keep]
+        out = dot(weights, jnp.concatenate(pairs + [blank_wide], axis=0))
+        mixed.append((out[:, 0:128] / out[:, 128:256]).astype(jnp.bfloat16))
     return jnp.concatenate(mixed, axis=1)
 
 
@@ -282,6 +288,7 @@
     scatter_ref,
     last_ref,
     rows_ref,
+    turned_ref,
     bias_ref,
     halo_ref,
     take_ref,
@@ -393,7 +400,7 @@
 
     for copy in prep:
         copy.wait()
-    prepare_bias(first, lat, lon, lat_count, lon_count, class_ref, table_ref, rows_ref, bias_ref)
+    prepare_bias(first, lat, lon, lat_count, lon_count, class_ref, table_ref, rows_ref, turned_ref, bias_ref)
     for copy in rest:
         copy.wait()
 
@@ -470,6 +477,7 @@
         pltpu.VMEM((4 * QROWS, 2 * TOK), bf16),
         pltpu.VMEM((GRID_ROWS, 4 * QROWS), bf16),
         pltpu.VMEM((2, 12, 16, KDIM), bf16),
+        pltpu.VMEM((2 * HEADS, TOK, 256), jnp.float32),
         pltpu.VMEM((2, TOK, 3 * GROUP), jnp.float32),
         pltpu.VMEM((MICRO, 4, QROWS, WIDTH), bf16),
         pltpu.VMEM((MICRO, 4, QROWS, WIDTH), bf16),
@@ -484,12 +492,12 @@
     ]
     result = pl.pallas_call(
         functools.partial(kernel, lat_count, lon_count),
-        out_shape=jax.ShapeDtypeStruct(fields.shape, bf16),
-        in_specs=[pl.BlockSpec(memory_space=pl.ANY)] * len(operands),
+        out_shape=pltpu.VMEM(fields.shape, bf16),
+        in_specs=[pl.BlockSpec(memory_space=pltpu.HBM)] * len(operands),
         out_specs=pl.BlockSpec(memory_space=pltpu.VMEM),
         scratch_shapes=scratch,
         compiler_params=pltpu.CompilerParams(
-            collective_id=0, has_side_effects=True, vmem_limit_bytes=63 * 1024 * 1024
+            collective_id=0, has_side_effects=True, vmem_limit_bytes=56 * 1024 * 1024
         ),
         name="two_blocks",
     )(*operands)

time: 40.8 us -> 37.5 us (0.919)
  Pallas kernels: 38.8 us -> 36.7 us
  local copies, waits for them, and re-layouts: 1.93 us -> 0.76 us
    pallas_call x1, Pallas kernels: 38.8 us -> 36.7 us  [body(): pl.pallas_call(functools.partial(kernel, lat_count, lon_count), out_shape...]
    unnamed x1, local copies, waits for them, and re-layouts: 1.93 us -> 0.76 us
where the time goes in v3:
time: 37.5 us
  Pallas kernels  36.7 us (98%)
  local copies, waits for them, and re-layouts  0.76 us (2%)
    pallas_call x1, Pallas kernels, body(): pl.pallas_call(functools.partial(kernel, lat_count, lon_count), out_shape...  36.7 us
    unnamed x1, local copies, waits for them, and re-layouts  0.76 us

profile of v3, /device:TPU:2, one launch (start us, length us, event | category | flops | bytes accessed | tf_op | source)
XLA Modules:
  0.0 37.5 jit_solution(3987623015652117998)
XLA Ops:
  0.0 36.7 %two_blocks.1 = bf16[2,6,12,4,384]{4,3,2,1,0:T(4,128)(2,1)S(1)} custom-call(bf16[2,6,12,4,384]{4,3,2,1,0:T(4,128)(2,1)} %bitcast.7, s32[4,24,384]{2,1,0:T(8,128)} %class_hbm.1, bf16[1,2,384]{2,1,0:T(2,128)(2,1)} %gains_hbm.1, bf16[1,384,1152]{2,1,0:T(8,128)(2,1)} %joint_hbm.1, bf16[1,384,384]{2,1,0:T(8,128)(2,1)} %oproj_hbm.1, ...), custom_call_target="tpu_custom_call" | custom-call | tf_op jit(solution)/shard_map/two_blocks/pallas_call | solution.py:493
  36.7 0.8 %copy.10 = bf16[1,2,4,6,12,384]{5,2,4,3,1,0:T(4,128)(2,1)} copy(bf16[1,2,4,6,12,384]{5,2,4,3,1,0:T(4,128)(2,1)S(1)} %bitcast.5) | data formatting | bytes 884736

commit v4 on v3

--- a/solution.py
+++ b/solution.py
@@ -16,7 +16,9 @@
 WIDTH = 384
 HEADS = 12
 FF = 1536
-QROWS = 80
+PIECES = 8
+PROWS = 112
+PACKED = 384
 GRID_ROWS = LEVELS * WIN_H * WIN_W
 GROUP = 640
 GUSED = 576
@@ -36,8 +38,10 @@
     return col, level, rest - level * 6
 
 
-def slot_row(row_half, col_half, level, row, col):
-    return (row_half + 2 * col_half) * QROWS + level * 18 + row * 6 + col
+def packed_row(window, row_half, col_half, level, row, col):
+    piece = window * 4 + row_half + 2 * col_half
+    inner = level * 18 + row * 6 + col
+    return jnp.where(inner < 32, piece * 32 + inner, 256 + piece * 16 + inner - 32)
 
 
 def halves(position, extent):
@@ -52,6 +56,13 @@
 
 def grid_place(row, col, level):
     return (row * 12 + col) * 4 + level
+
+
+def pack_matrix(target):
+    row = lax.broadcasted_iota(jnp.int32, (PACKED, 1), 0)
+    last = jnp.where((row & 12) == 12, -1, row - (row & 12))
+    row = jnp.where(row < 256, row, last)
+    return (row == target).astype(jnp.float32).astype(jnp.bfloat16)
 
 
 def gather_matrix():
@@ -61,7 +72,7 @@
     row_half, row_in = halves(row, 3)
     col_half, col_in = halves(pair - row * 12, 6)
     level = ((place & 3) + 3) & 3
-    return one_hot(4 * QROWS, slot_row(1 - row_half, 1 - col_half, level, row_in, col_in))
+    return pack_matrix(packed_row(level >> 1, 1 - row_half, 1 - col_half, level & 1, row_in, col_in))
 
 
 def scatter_matrix():
@@ -70,21 +81,22 @@
     col, level, row = token_parts(rest)
     row_half, row_in = halves(row, 3)
     col_half, col_in = halves(col, 6)
-    return one_hot(4 * QROWS, slot_row(row_half, col_half, 2 * window + level, row_in, col_in))
-
-
-def slot_parts():
-    place = lax.broadcasted_iota(jnp.int32, (1, 4 * QROWS), 1)
-    slot = divide(place, QROWS)
-    rest = place - slot * QROWS
-    level = divide(rest, 18)
-    inner = rest - level * 18
-    row = divide(inner, 6)
-    return rest < 72, slot & 1, slot >> 1, level, row, inner - row * 6
+    return pack_matrix(packed_row(window, row_half, col_half, level, row_in, col_in))
+
+
+def packed_parts():
+    place = lax.broadcasted_iota(jnp.int32, (1, PACKED), 1)
+    early = place < 256
+    piece = jnp.where(early, place >> 5, (place - 256) >> 4)
+    inner = jnp.where(early, place & 31, 32 + (place & 3))
+    used = early | ((place & 12) != 12)
+    level, rest = halves(inner, 18)
+    row = divide(rest, 6)
+    return used, piece & 1, (piece >> 1) & 1, 2 * (piece >> 2) + level, row, rest - row * 6
 
 
 def into_matrix(one):
-    used, row_half, col_half, level, row, col = slot_parts()
+    used, row_half, col_half, level, row, col = packed_parts()
     row = row + 3 * (row_half * one + (1 - row_half) * (1 - one))
     col = col + 6 * (col_half * one + (1 - col_half) * (1 - one))
     level = (level + 1 - one) & 3
@@ -93,7 +105,7 @@
 
 
 def back_matrix():
-    used, row_half, col_half, level, row, col = slot_parts()
+    used, row_half, col_half, level, row, col = packed_parts()
     place = grid_place(row + 3 * (1 - row_half), col + 6 * (1 - col_half), (level + 1) & 3)
     return one_hot(GRID_ROWS, jnp.where(used, place, -1))
 
@@ -105,6 +117,30 @@
     return one_hot(GRID_ROWS, grid_place(row, col, 2 * window + level))
 
 
+def pack(rows, refs, m):
+    rows = rows.astype(jnp.bfloat16)
+    chunk = (lax.broadcasted_iota(jnp.int32, (16 * PIECES, 1), 0) >> 2) & 3
+    last = rows[256:].astype(jnp.float32)
+    last = jnp.where(chunk == 0, last[:, 0:128], jnp.where(chunk == 1, last[:, 128:256], last[:, 256:384]))
+    last = last.astype(jnp.bfloat16)
+    for piece in range(PIECES):
+        for ref in refs[piece]:
+            for c in range(3):
+                ref[m, piece, c * 32 : c * 32 + 32, :] = rows[piece * 32 : piece * 32 + 32, c * 128 : c * 128 + 128]
+            ref[m, piece, 96:112, :] = last[piece * 16 : piece * 16 + 16]
+
+
+def unpack(ref, m):
+    chunk = (lax.broadcasted_iota(jnp.int32, (16 * PIECES, 1), 0) >> 2) & 3
+    rows = [
+        jnp.concatenate([ref[m, piece, c * 32 : c * 32 + 32, :] for c in range(3)], axis=1)
+        for piece in range(PIECES)
+    ]
+    last = jnp.concatenate([ref[m, piece, 96:112, :] for piece in range(PIECES)], axis=0).astype(jnp.float32)
+    last = jnp.concatenate([jnp.where(chunk == c, last, 0.0) for c in range(3)], axis=1)
+    return jnp.concatenate(rows + [last.astype(jnp.bfloat16)], axis=0)
+
+
 def dot(a, b):
     return jnp.dot(a, b, preferred_element_type=jnp.float32)
 
@@ -131,9 +167,13 @@
 
 def prepare_bias(first, lat, lon, lat_count, lon_count, class_ref, table_ref, rows_ref, turned_ref, bias_ref):
     kinds = 2 * lat_count
+    one = jnp.where(first, 1, 0)
+    lats = (lat, lax.rem(lat + lat_count - one, lat_count))
+    lons = (lon, lax.rem(lon + lon_count - one, lon_count))
     to_row = lax.broadcasted_iota(jnp.int32, (32, HEADS * kinds), 0)
     to_col = lax.broadcasted_iota(jnp.int32, (32, HEADS * kinds), 1)
-    wanted = (to_row & 15) * kinds + (to_row >> 4) * lat_count + lat
+    kind = jnp.where(to_row < 16, lat, lat_count + lats[1])
+    wanted = (to_row & 15) * kinds + kind
     own = (to_col == wanted).astype(jnp.float32).astype(jnp.bfloat16)
     table = dot(own, table_ref[...].reshape(HEADS * kinds, -1)).astype(jnp.bfloat16)
     rows_ref[...] = jnp.zeros_like(rows_ref)
@@ -164,9 +204,6 @@
                 turned_ref[i * HEADS + h, cb * 12 : cb * 12 + 12, :] = spread[start : start + 12]
     rows_all = 6 * lat_count
     cols_all = 12 * lon_count
-    one = jnp.where(first, 1, 0)
-    row_start = lat * 6 + 3 * one
-    col_start = lon * 12 + 6 * one
     classes = class_ref[...].reshape(LEVELS * rows_all, cols_all).astype(jnp.float32).astype(jnp.bfloat16)
     col_b, level_b, row_b = token_parts(lax.broadcasted_iota(jnp.int32, (TOK, 1), 0))
 
@@ -176,27 +213,29 @@
     def onehot(a, b):
         return (a == b).astype(jnp.float32).astype(jnp.bfloat16)
 
-    across = dot(
-        classes,
-        onehot(lax.broadcasted_iota(jnp.int32, (cols_all, 256), 0), wrap(col_start + col_a, cols_all)),
-    )
-    down = dot_nt(
-        onehot(lax.broadcasted_iota(jnp.int32, (TOK, cols_all), 1), wrap(col_start + col_b, cols_all)),
-        classes,
-    )
     identity = (
         lax.broadcasted_iota(jnp.int32, (TOK, 256), 0) == lax.broadcasted_iota(jnp.int32, (TOK, 256), 1)
     )
     identity = identity.astype(jnp.float32).astype(jnp.bfloat16)
-    place_a = lax.broadcasted_iota(jnp.int32, across.shape, 0)
-    place_b = lax.broadcasted_iota(jnp.int32, down.shape, 1)
+    place_a = lax.broadcasted_iota(jnp.int32, (LEVELS * rows_all, 256), 0)
+    place_b = lax.broadcasted_iota(jnp.int32, (TOK, LEVELS * rows_all), 1)
     for i in range(2):
+        row_start = lats[i] * 6 + 3 * one
+        col_start = lons[i] * 12 + 6 * one
+        across = dot(
+            classes,
+            onehot(lax.broadcasted_iota(jnp.int32, (cols_all, 256), 0), wrap(col_start + col_a, cols_all)),
+        )
+        down = dot_nt(
+            onehot(lax.broadcasted_iota(jnp.int32, (TOK, cols_all), 1), wrap(col_start + col_b, cols_all)),
+            classes,
+        )
 
         def region(place, level, row, values, axis):
             at = ((2 * i + level + one) & 3) * rows_all + wrap(row_start + row, rows_all)
             value = jnp.sum(jnp.where(place == at, values, 0.0), axis=axis, keepdims=True)
             flags = 2 * (2 * i + level >= 3).astype(jnp.int32)
-            flags = flags + (lat * 6 + row >= rows_all - 3).astype(jnp.int32)
+            flags = flags + (lats[i] * 6 + row >= rows_all - 3).astype(jnp.int32)
             return 4.0 * value + (one * flags).astype(jnp.float32)
 
         region_a = region(place_a, level_a, row_a, across, 0)
@@ -309,20 +348,27 @@
     lat_down = lax.rem(lat + lat_count - 1, lat_count)
     lon_up = lax.rem(lon + 1, lon_count)
     lon_down = lax.rem(lon + lon_count - 1, lon_count)
-    behind = [(lat, lon), (lat_down, lon), (lat, lon_down), (lat_down, lon_down)]
-    ahead = [(lat, lon), (lat_up, lon), (lat, lon_up), (lat_up, lon_up)]
+    own = (0, 7)
+    others = (3, 4, 2, 5, 1, 6)
+
+    def owner(piece, sign):
+        row_half, col_half, window = piece & 1, (piece >> 1) & 1, piece >> 2
+        up, right = sign * (row_half - window), sign * (col_half - window)
+        where_lat = {0: lat, 1: lat_up, -1: lat_down}[up]
+        where_lon = {0: lon, 1: lon_up, -1: lon_down}[right]
+        return (where_lat, where_lon)
 
     barrier = pltpu.get_barrier_semaphore()
 
     @pl.when(first)
     def _():
-        for where in behind[1:] + ahead[1:]:
-            pl.semaphore_signal(barrier, inc=1, device_id=(0,) + where, device_id_type=MESH)
+        for piece in others:
+            pl.semaphore_signal(barrier, inc=1, device_id=(0,) + owner(piece, 1), device_id_type=MESH)
 
     @pl.when(jnp.logical_not(first))
     def _():
-        for where in behind:
-            pl.semaphore_signal(barrier, inc=1, device_id=(0,) + where, device_id_type=MESH)
+        for piece in others + own[:1]:
+            pl.semaphore_signal(barrier, inc=1, device_id=(0,) + owner(piece, 1), device_id_type=MESH)
 
     loads = []
 
@@ -348,7 +394,7 @@
             dst_ref=take_ref.at[m, q],
             send_sem=halo_send.at[m, q],
             recv_sem=take_recv.at[m, q],
-            device_id=(0,) + behind[q],
+            device_id=(0,) + owner(q, -1),
             device_id_type=MESH,
         )
 
@@ -358,7 +404,7 @@
             dst_ref=home_ref.at[m, q],
             send_sem=home_send.at[m, q],
             recv_sem=home_recv.at[m, q],
-            device_id=(0,) + ahead[q],
+            device_id=(0,) + owner(q, 1),
             device_id_type=MESH,
         )
 
@@ -368,7 +414,7 @@
             dst_ref=take_ref.at[m, q],
             send_sem=next_send.at[m, q],
             recv_sem=take_recv.at[m, q],
-            device_id=(1,) + ahead[q],
+            device_id=(1,) + owner(q, 1),
             device_id_type=MESH,
         )
 
@@ -378,13 +424,11 @@
     def _():
         gather = gather_matrix()
         for m in range(MICRO):
-            sorted_rows = dot(gather, fields_ref[m].reshape(GRID_ROWS, WIDTH)).astype(jnp.bfloat16)
-            take_ref[m, 0] = sorted_rows[0:QROWS]
-            for q in range(1, 4):
-                halo_ref[m, q] = sorted_rows[q * QROWS : (q + 1) * QROWS]
+            rows = dot(gather, fields_ref[m].reshape(GRID_ROWS, WIDTH))
+            pack(rows, [[take_ref] if q in own else [halo_ref] for q in range(PIECES)], m)
             if m == 0:
-                pl.semaphore_wait(barrier, 10)
-            for q in (3, 2, 1):
+                pl.semaphore_wait(barrier, 13)
+            for q in others:
                 halo_copy(m, q).start()
 
     into_ref[...] = into_matrix(jnp.where(first, 1, 0))
@@ -407,25 +451,27 @@
     def step(m, carry):
         @pl.when(first)
         def _():
-            for q in range(1, 4):
+            for q in others:
                 halo_copy(m, q).wait_recv()
 
         @pl.when(jnp.logical_not(first))
         def _():
-            for q in range(4):
+            for q in range(PIECES):
                 next_copy(m, q).wait_recv()
 
-        x = dot(into_ref[...], take_ref[m].reshape(4 * QROWS, WIDTH))
+        x = dot(into_ref[...], unpack(take_ref, m))
         y = block(x, gains_ref, joint_ref, oproj_ref, expand_ref, reduce_ref, bias_ref)
 
         @pl.when(first)
         def _():
-            pieces = dot(scatter_ref[...], y).astype(jnp.bfloat16)
-            done_ref[m] = pieces.reshape(4, QROWS, WIDTH)
-            home_ref[m, 0] = pieces[0:QROWS]
-            for q in (3, 2, 1, 0):
+            pack(
+                dot(scatter_ref[...], y),
+                [[done_ref, home_ref] if q in own else [done_ref] for q in range(PIECES)],
+                m,
+            )
+            for q in others + own:
                 next_copy(m, q).start()
-            for q in (3, 2, 1):
+            for q in others:
                 home_copy(m, q).start()
 
         @pl.when(jnp.logical_not(first))
@@ -442,14 +488,14 @@
     @pl.when(first)
     def _():
         for m in range(MICRO):
-            for q in range(1, 4):
+            for q in others:
                 home_copy(m, q).wait_recv()
-            write(m, dot(last_ref[...], home_ref[m].reshape(4 * QROWS, WIDTH)).astype(jnp.bfloat16))
+            write(m, dot(last_ref[...], unpack(home_ref, m)).astype(jnp.bfloat16))
         for m in range(MICRO):
-            for q in range(1, 4):
+            for q in others:
                 halo_copy(m, q).wait_send()
                 home_copy(m, q).wait_send()
-            for q in range(4):
+            for q in range(PIECES):
                 next_copy(m, q).wait_send()
 
 
@@ -473,22 +519,22 @@
         pltpu.VMEM((WIDTH, FF), bf16),
         pltpu.VMEM((FF, WIDTH), bf16),
         pltpu.VMEM((HEADS,) + earth_bias.shape[1:2] + earth_bias.shape[3:], bf16),
-        pltpu.VMEM((2 * TOK, 4 * QROWS), bf16),
-        pltpu.VMEM((4 * QROWS, 2 * TOK), bf16),
-        pltpu.VMEM((GRID_ROWS, 4 * QROWS), bf16),
+        pltpu.VMEM((2 * TOK, PACKED), bf16),
+        pltpu.VMEM((PACKED, 2 * TOK), bf16),
+        pltpu.VMEM((GRID_ROWS, PACKED), bf16),
         pltpu.VMEM((2, 12, 16, KDIM), bf16),
         pltpu.VMEM((2 * HEADS, TOK, 256), jnp.float32),
         pltpu.VMEM((2, TOK, 3 * GROUP), jnp.float32),
-        pltpu.VMEM((MICRO, 4, QROWS, WIDTH), bf16),
-        pltpu.VMEM((MICRO, 4, QROWS, WIDTH), bf16),
-        pltpu.VMEM((MICRO, 4, QROWS, WIDTH), bf16),
-        pltpu.VMEM((MICRO, 4, QROWS, WIDTH), bf16),
+        pltpu.VMEM((MICRO, PIECES, PROWS, 128), bf16),
+        pltpu.VMEM((MICRO, PIECES, PROWS, 128), bf16),
+        pltpu.VMEM((MICRO, PIECES, PROWS, 128), bf16),
+        pltpu.VMEM((MICRO, PIECES, PROWS, 128), bf16),
         pltpu.SemaphoreType.DMA((14,)),
-        pltpu.SemaphoreType.DMA((MICRO, 4)),
-        pltpu.SemaphoreType.DMA((MICRO, 4)),
-        pltpu.SemaphoreType.DMA((MICRO, 4)),
-        pltpu.SemaphoreType.DMA((MICRO, 4)),
-        pltpu.SemaphoreType.DMA((MICRO, 4)),
+        pltpu.SemaphoreType.DMA((MICRO, PIECES)),
+        pltpu.SemaphoreType.DMA((MICRO, PIECES)),
+        pltpu.SemaphoreType.DMA((MICRO, PIECES)),
+        pltpu.SemaphoreType.DMA((MICRO, PIECES)),
+        pltpu.SemaphoreType.DMA((MICRO, PIECES)),
     ]
     result = pl.pallas_call(
         functools.partial(kernel, lat_count, lon_count),

time: 37.5 us -> 35.3 us (0.941)
  Pallas kernels: 36.7 us -> 34.4 us
    pallas_call x1, Pallas kernels: 36.7 us -> 34.4 us  [body(): pl.pallas_call(functools.partial(kernel, lat_count, lon_count), out_shape...]
where the time goes in v4:
time: 35.3 us; the launch traced here: 35.2 us
  Pallas kernels  34.4 us (97%)
  local copies, waits for them, and re-layouts  0.76 us (2%)
    pallas_call x1, Pallas kernels, body(): pl.pallas_call(functools.partial(kernel, lat_count, lon_count), out_shape...  34.4 us
    unnamed x1, local copies, waits for them, and re-layouts  0.76 us

profile of v4, /device:TPU:2, one launch (start us, length us, event | category | flops | bytes accessed | tf_op | source)
XLA Modules:
  0.0 35.2 jit_solution(13137765593182193818)
XLA Ops:
  0.0 34.4 %two_blocks.1 = bf16[2,6,12,4,384]{4,3,2,1,0:T(4,128)(2,1)S(1)} custom-call(bf16[2,6,12,4,384]{4,3,2,1,0:T(4,128)(2,1)} %bitcast.7, s32[4,24,384]{2,1,0:T(8,128)} %class_hbm.1, bf16[1,2,384]{2,1,0:T(2,128)(2,1)} %gains_hbm.1, bf16[1,384,1152]{2,1,0:T(8,128)(2,1)} %joint_hbm.1, bf16[1,384,384]{2,1,0:T(8,128)(2,1)} %oproj_hbm.1, ...), custom_call_target="tpu_custom_call" | custom-call | tf_op jit(solution)/shard_map/two_blocks/pallas_call | solution.py:539
  34.4 0.8 %copy.10 = bf16[1,2,4,6,12,384]{5,2,4,3,1,0:T(4,128)(2,1)} copy(bf16[1,2,4,6,12,384]{5,2,4,3,1,0:T(4,128)(2,1)S(1)} %bitcast.5) | data formatting | bytes 884736

commit v5 on v4

--- a/solution.py
+++ b/solution.py
@@ -18,7 +18,7 @@
 FF = 1536
 PIECES = 8
 PROWS = 112
-PACKED = 384
+PACKED = 192
 GRID_ROWS = LEVELS * WIN_H * WIN_W
 GROUP = 640
 GUSED = 576
@@ -39,9 +39,9 @@
 
 
 def packed_row(window, row_half, col_half, level, row, col):
-    piece = window * 4 + row_half + 2 * col_half
+    quarter = row_half + 2 * col_half
     inner = level * 18 + row * 6 + col
-    return jnp.where(inner < 32, piece * 32 + inner, 256 + piece * 16 + inner - 32)
+    return window * PACKED + jnp.where(inner < 32, quarter * 32 + inner, 96 + quarter * 16 + inner)
 
 
 def halves(position, extent):
@@ -58,10 +58,10 @@
     return (row * 12 + col) * 4 + level
 
 
-def pack_matrix(target):
-    row = lax.broadcasted_iota(jnp.int32, (PACKED, 1), 0)
+def pack_matrix(rows, target):
+    row = lax.broadcasted_iota(jnp.int32, (rows, 1), 0)
     last = jnp.where((row & 12) == 12, -1, row - (row & 12))
-    row = jnp.where(row < 256, row, last)
+    row = jnp.where(halves(row, PACKED)[1] < 128, row, last)
     return (row == target).astype(jnp.float32).astype(jnp.bfloat16)
 
 
@@ -72,42 +72,49 @@
     row_half, row_in = halves(row, 3)
     col_half, col_in = halves(pair - row * 12, 6)
     level = ((place & 3) + 3) & 3
-    return pack_matrix(packed_row(level >> 1, 1 - row_half, 1 - col_half, level & 1, row_in, col_in))
+    target = packed_row(level >> 1, 1 - row_half, 1 - col_half, level & 1, row_in, col_in)
+    return pack_matrix(2 * PACKED, target)
 
 
 def scatter_matrix():
-    token = lax.broadcasted_iota(jnp.int32, (1, 2 * TOK), 1)
-    window, rest = halves(token, TOK)
-    col, level, row = token_parts(rest)
+    col, level, row = token_parts(lax.broadcasted_iota(jnp.int32, (1, TOK), 1))
     row_half, row_in = halves(row, 3)
     col_half, col_in = halves(col, 6)
-    return pack_matrix(packed_row(window, row_half, col_half, level, row_in, col_in))
-
-
-def packed_parts():
-    place = lax.broadcasted_iota(jnp.int32, (1, PACKED), 1)
-    early = place < 256
-    piece = jnp.where(early, place >> 5, (place - 256) >> 4)
+    return pack_matrix(PACKED, packed_row(0, row_half, col_half, level, row_in, col_in))
+
+
+def packed_parts(rows):
+    place = lax.broadcasted_iota(jnp.int32, (1, rows), 1)
+    window, place = halves(place, PACKED)
+    early = place < 128
+    quarter = jnp.where(early, place >> 5, (place - 128) >> 4)
     inner = jnp.where(early, place & 31, 32 + (place & 3))
     used = early | ((place & 12) != 12)
     level, rest = halves(inner, 18)
     row = divide(rest, 6)
-    return used, piece & 1, (piece >> 1) & 1, 2 * (piece >> 2) + level, row, rest - row * 6
-
-
-def into_matrix(one):
-    used, row_half, col_half, level, row, col = packed_parts()
-    row = row + 3 * (row_half * one + (1 - row_half) * (1 - one))
-    col = col + 6 * (col_half * one + (1 - col_half) * (1 - one))
-    level = (level + 1 - one) & 3
+    return used, quarter & 1, quarter >> 1, 2 * window + level, row, rest - row * 6
+
+
+def shifted_matrix():
+    used, row_half, col_half, level, row, col = packed_parts(PACKED)
+    token = (col + 6 * col_half) * 12 + level * 6 + row + 3 * row_half
+    return one_hot(TOK, jnp.where(used, token, -1))
+
+
+def owned_parts():
+    used, row_half, col_half, level, row, col = packed_parts(2 * PACKED)
+    return used, (level + 1) & 3, row + 3 * (1 - row_half), col + 6 * (1 - col_half)
+
+
+def owned_matrix():
+    used, level, row, col = owned_parts()
     token = (level >> 1) * TOK + col * 12 + (level & 1) * 6 + row
     return one_hot(2 * TOK, jnp.where(used, token, -1))
 
 
 def back_matrix():
-    used, row_half, col_half, level, row, col = packed_parts()
-    place = grid_place(row + 3 * (1 - row_half), col + 6 * (1 - col_half), (level + 1) & 3)
-    return one_hot(GRID_ROWS, jnp.where(used, place, -1))
+    used, level, row, col = owned_parts()
+    return one_hot(GRID_ROWS, jnp.where(used, grid_place(row, col, level), -1))
 
 
 def plain_matrix():
@@ -117,28 +124,34 @@
     return one_hot(GRID_ROWS, grid_place(row, col, 2 * window + level))
 
 
-def pack(rows, refs, m):
+def pack(rows, refs, m, window):
     rows = rows.astype(jnp.bfloat16)
-    chunk = (lax.broadcasted_iota(jnp.int32, (16 * PIECES, 1), 0) >> 2) & 3
-    last = rows[256:].astype(jnp.float32)
+    chunk = (lax.broadcasted_iota(jnp.int32, (64, 1), 0) >> 2) & 3
+    last = rows[128:].astype(jnp.float32)
     last = jnp.where(chunk == 0, last[:, 0:128], jnp.where(chunk == 1, last[:, 128:256], last[:, 256:384]))
     last = last.astype(jnp.bfloat16)
-    for piece in range(PIECES):
+    for quarter in range(4):
+        piece = window * 4 + quarter
         for ref in refs[piece]:
             for c in range(3):
-                ref[m, piece, c * 32 : c * 32 + 32, :] = rows[piece * 32 : piece * 32 + 32, c * 128 : c * 128 + 128]
-            ref[m, piece, 96:112, :] = last[piece * 16 : piece * 16 + 16]
-
-
-def unpack(ref, m):
-    chunk = (lax.broadcasted_iota(jnp.int32, (16 * PIECES, 1), 0) >> 2) & 3
+                ref[m, piece, c * 32 : c * 32 + 32, :] = rows[quarter * 32 : quarter * 32 + 32, c * 128 : c * 128 + 128]
+            ref[m, piece, 96:112, :] = last[quarter * 16 : quarter * 16 + 16]
+
+
+def unpack(ref, m, window):
+    chunk = (lax.broadcasted_iota(jnp.int32, (64, 1), 0) >> 2) & 3
+    pieces = range(window * 4, window * 4 + 4)
     rows = [
         jnp.concatenate([ref[m, piece, c * 32 : c * 32 + 32, :] for c in range(3)], axis=1)
-        for piece in range(PIECES)
+        for piece in pieces
     ]
-    last = jnp.concatenate([ref[m, piece, 96:112, :] for piece in range(PIECES)], axis=0).astype(jnp.float32)
+    last = jnp.concatenate([ref[m, piece, 96:112, :] for piece in pieces], axis=0).astype(jnp.float32)
     last = jnp.concatenate([jnp.where(chunk == c, last, 0.0) for c in range(3)], axis=1)
     return jnp.concatenate(rows + [last.astype(jnp.bfloat16)], axis=0)
+
+
+def unpack_both(ref, m):
+    return jnp.concatenate([unpack(ref, m, window) for window in range(2)], axis=0)
 
 
 def dot(a, b):
@@ -326,6 +339,8 @@
     into_ref,
     scatter_ref,
     last_ref,
+    x_ref,
+    y_ref,
     rows_ref,
     turned_ref,
     bias_ref,
@@ -339,6 +354,7 @@
     home_send,
     home_recv,
     next_send,
+    hand_send,
 ):
     sec = lax.axis_index("section")
     lat = lax.axis_index("lat")
@@ -364,6 +380,7 @@
     def _():
         for piece in others:
             pl.semaphore_signal(barrier, inc=1, device_id=(0,) + owner(piece, 1), device_id_type=MESH)
+        pl.semaphore_signal(barrier, inc=1, device_id=(1, lat, lon), device_id_type=MESH)
 
     @pl.when(jnp.logical_not(first))
     def _():
@@ -408,6 +425,32 @@
             device_id_type=MESH,
         )
 
+    odd = lax.rem(lat, 2)
+    lat_chip = lat + 1 - 2 * odd
+    lon_chip = (lax.rem(lon + lon_count - odd, lon_count), lax.rem(lon + 1 - odd, lon_count))
+
+    def chip_copy(m, col_half):
+        piece = 1 + 3 * odd + 2 * col_half
+        return pltpu.make_async_remote_copy(
+            src_ref=done_ref.at[m, piece],
+            dst_ref=home_ref.at[m, piece],
+            send_sem=home_send.at[m, piece],
+            recv_sem=home_recv.at[m, piece],
+            device_id=(0, lat_chip, lon_chip[col_half]),
+            device_id_type=MESH,
+        )
+
+    def hand_copy(m, col_half):
+        piece = 1 + 3 * odd + 2 * col_half
+        return pltpu.make_async_remote_copy(
+            src_ref=take_ref.at[m, piece],
+            dst_ref=home_ref.at[m, piece],
+            send_sem=hand_send.at[m, col_half],
+            recv_sem=home_recv.at[m, piece],
+            device_id=(0, lat, lon),
+            device_id_type=MESH,
+        )
+
     def next_copy(m, q):
         return pltpu.make_async_remote_copy(
             src_ref=done_ref.at[m, q],
@@ -425,22 +468,25 @@
         gather = gather_matrix()
         for m in range(MICRO):
             rows = dot(gather, fields_ref[m].reshape(GRID_ROWS, WIDTH))
-            pack(rows, [[take_ref] if q in own else [halo_ref] for q in range(PIECES)], m)
+            refs = [[take_ref] if q in own else [halo_ref] for q in range(PIECES)]
+            for window in range(2):
+                pack(rows[window * PACKED : (window + 1) * PACKED], refs, m, window)
             if m == 0:
                 pl.semaphore_wait(barrier, 13)
             for q in others:
                 halo_copy(m, q).start()
 
-    into_ref[...] = into_matrix(jnp.where(first, 1, 0))
-
     @pl.when(first)
     def _():
+        into_ref[0:TOK, 0:PACKED] = shifted_matrix()
         scatter_ref[...] = scatter_matrix()
         last_ref[...] = back_matrix()
 
     @pl.when(jnp.logical_not(first))
     def _():
+        into_ref[...] = owned_matrix()
         last_ref[:, 0 : 2 * TOK] = plain_matrix()
+        pl.semaphore_wait(barrier, 1)
 
     for copy in prep:
         copy.wait()
@@ -453,30 +499,37 @@
         def _():
             for q in others:
                 halo_copy(m, q).wait_recv()
+            for window in range(2):
+                rows = dot(into_ref[0:TOK, 0:PACKED], unpack(take_ref, m, window))
+                x_ref[window * TOK : (window + 1) * TOK, :] = rows.astype(jnp.bfloat16)
 
         @pl.when(jnp.logical_not(first))
         def _():
             for q in range(PIECES):
                 next_copy(m, q).wait_recv()
-
-        x = dot(into_ref[...], unpack(take_ref, m))
-        y = block(x, gains_ref, joint_ref, oproj_ref, expand_ref, reduce_ref, bias_ref)
+            for col_half in range(2):
+                hand_copy(m, col_half).start()
+            x_ref[...] = dot(into_ref[...], unpack_both(take_ref, m)).astype(jnp.bfloat16)
+
+        x = x_ref[...].astype(jnp.float32)
+        y_ref[...] = block(x, gains_ref, joint_ref, oproj_ref, expand_ref, reduce_ref, bias_ref)
 
         @pl.when(first)
         def _():
-            pack(
-                dot(scatter_ref[...], y),
-                [[done_ref, home_ref] if q in own else [done_ref] for q in range(PIECES)],
-                m,
-            )
+            refs = [[done_ref, home_ref] if q in own else [done_ref] for q in range(PIECES)]
+            for window in range(2):
+                y = y_ref[window * TOK : (window + 1) * TOK, :]
+                pack(dot(scatter_ref[...], y), refs, m, window)
             for q in others + own:
                 next_copy(m, q).start()
-            for q in others:
+            for q in (2, 5):
                 home_copy(m, q).start()
+            for col_half in range(2):
+                chip_copy(m, col_half).start()
 
         @pl.when(jnp.logical_not(first))
         def _():
-            write(m, dot(last_ref[:, 0 : 2 * TOK], y).astype(jnp.bfloat16))
+            write(m, dot(last_ref[:, 0 : 2 * TOK], y_ref[...]).astype(jnp.bfloat16))
 
         return carry
 
@@ -490,13 +543,22 @@
         for m in range(MICRO):
             for q in others:
                 home_copy(m, q).wait_recv()
-            write(m, dot(last_ref[...], unpack(home_ref, m)).astype(jnp.bfloat16))
+            write(m, dot(last_ref[...], unpack_both(home_ref, m)).astype(jnp.bfloat16))
         for m in range(MICRO):
             for q in others:
                 halo_copy(m, q).wait_send()
+            for q in (2, 5):
                 home_copy(m, q).wait_send()
+            for col_half in range(2):
+                chip_copy(m, col_half).wait_send()
             for q in range(PIECES):
                 next_copy(m, q).wait_send()
+
+    @pl.when(jnp.logical_not(first))
+    def _():
+        for m in range(MICRO):
+            for col_half in range(2):
+                hand_copy(m, col_half).wait_send()
 
 
 def body(
@@ -519,9 +581,11 @@
         pltpu.VMEM((WIDTH, FF), bf16),
         pltpu.VMEM((FF, WIDTH), bf16),
         pltpu.VMEM((HEADS,) + earth_bias.shape[1:2] + earth_bias.shape[3:], bf16),
-        pltpu.VMEM((2 * TOK, PACKED), bf16),
-        pltpu.VMEM((PACKED, 2 * TOK), bf16),
-        pltpu.VMEM((GRID_ROWS, PACKED), bf16),
+        pltpu.VMEM((2 * TOK, 2 * PACKED), bf16),
+        pltpu.VMEM((PACKED, TOK), bf16),
+        pltpu.VMEM((GRID_ROWS, 2 * PACKED), bf16),
+        pltpu.VMEM((2 * TOK, WIDTH), bf16),
+        pltpu.VMEM((2 * TOK, WIDTH), bf16),
         pltpu.VMEM((2, 12, 16, KDIM), bf16),
         pltpu.VMEM((2 * HEADS, TOK, 256), jnp.float32),
         pltpu.VMEM((2, TOK, 3 * GROUP), jnp.float32),
@@ -535,6 +599,7 @@
         pltpu.SemaphoreType.DMA((MICRO, PIECES)),
         pltpu.SemaphoreType.DMA((MICRO, PIECES)),
         pltpu.SemaphoreType.DMA((MICRO, PIECES)),
+        pltpu.SemaphoreType.DMA((MICRO, 2)),
     ]
     result = pl.pallas_call(
         functools.partial(kernel, lat_count, lon_count),

time: 35.3 us -> 34.8 us (0.986)
  the two profiles are of different devices: /device:TPU:2 before, /device:TPU:1 now
where the time goes in v5:
time: 34.8 us
  Pallas kernels  34 us (98%)
  local copies, waits for them, and re-layouts  0.76 us (2%)
    pallas_call x1, Pallas kernels, body(): pl.pallas_call(functools.partial(kernel, lat_count, lon_count), out_shape...  34 us
    unnamed x1, local copies, waits for them, and re-layouts  0.76 us

profile of v5, /device:TPU:1, one launch (start us, length us, event | category | flops | bytes accessed | tf_op | source)
XLA Modules:
  0.0 34.8 jit_solution(13238598580378326329)
XLA Ops:
  0.0 34.0 %two_blocks.1 = bf16[2,6,12,4,384]{4,3,2,1,0:T(4,128)(2,1)S(1)} custom-call(bf16[2,6,12,4,384]{4,3,2,1,0:T(4,128)(2,1)} %bitcast.7, s32[4,24,384]{2,1,0:T(8,128)} %class_hbm.1, bf16[1,2,384]{2,1,0:T(2,128)(2,1)} %gains_hbm.1, bf16[1,384,1152]{2,1,0:T(8,128)(2,1)} %joint_hbm.1, bf16[1,384,384]{2,1,0:T(8,128)(2,1)} %oproj_hbm.1, ...), custom_call_target="tpu_custom_call" | custom-call | tf_op jit(solution)/shard_map/two_blocks/pallas_call | solution.py:604
  34.0 0.8 %copy.10 = bf16[1,2,4,6,12,384]{5,2,4,3,1,0:T(4,128)(2,1)} copy(bf16[1,2,4,6,12,384]{5,2,4,3,1,0:T(4,128)(2,1)S(1)} %bitcast.5) | data formatting | bytes 884736

commit v6 on v5

--- a/solution.py
+++ b/solution.py
@@ -295,25 +295,23 @@
     return jnp.concatenate(mixed, axis=1)
 
 
-def block(x, gains_ref, joint_ref, out_ref, expand_ref, reduce_ref, bias_ref):
-    gains = gains_ref[...].astype(jnp.float32)
-    normed = layer_norm(x, gains[0:1]).astype(jnp.bfloat16)
+def project(x, gains_ref, joint_ref):
+    normed = layer_norm(x, gains_ref[0:1].astype(jnp.float32)).astype(jnp.bfloat16)
     projected = dot(normed, joint_ref[...])
-    query = (projected[:, 0:WIDTH] * (LOG2E * 32**-0.5)).astype(jnp.bfloat16)
-    key = projected[:, WIDTH : 2 * WIDTH].astype(jnp.bfloat16)
-    value = projected[:, 2 * WIDTH :].astype(jnp.bfloat16)
+    query = projected[:, 0:WIDTH] * (LOG2E * 32**-0.5)
+    return jnp.concatenate([query, projected[:, WIDTH:]], axis=1).astype(jnp.bfloat16)
+
+
+def finish(x, projected, gains_ref, out_ref, expand_ref, reduce_ref, bias_ref):
+    query, key, value = (projected[:, n * WIDTH : (n + 1) * WIDTH] for n in range(3))
     mixed = []
     for i in range(2):
-        rows = slice(i * TOK, i * TOK + TOK)
+        rows = slice(i * TOK, (i + 1) * TOK)
         mixed.append(attention(query[rows], key[rows], value[rows], bias_ref, i))
     hidden = x + dot(jnp.concatenate(mixed, axis=0), out_ref[...])
-    again = layer_norm(hidden, gains[1:2]).astype(jnp.bfloat16)
-    total = hidden
-    step = 512
-    for start in range(0, FF, step):
-        act = gelu(dot(again, expand_ref[:, start : start + step])).astype(jnp.bfloat16)
-        total = total + dot(act, reduce_ref[start : start + step, :])
-    return total.astype(jnp.bfloat16)
+    again = layer_norm(hidden, gains_ref[1:2].astype(jnp.float32)).astype(jnp.bfloat16)
+    act = gelu(dot(again, expand_ref[...])).astype(jnp.bfloat16)
+    return (hidden + dot(act, reduce_ref[...])).astype(jnp.bfloat16)
 
 
 def kernel(
@@ -336,6 +334,7 @@
     expand_ref,
     reduce_ref,
     table_ref,
+    gather_ref,
     into_ref,
     scatter_ref,
     last_ref,
@@ -395,7 +394,7 @@
         loads.append(copy)
         return copy
 
-    load_fields = load(fields_hbm, fields_ref)
+    load_fields = [load(fields_hbm.at[m], fields_ref.at[m]) for m in range(MICRO)]
     prep = [load(table_hbm.at[0], table_ref), load(class_hbm, class_ref)]
     rest = [
         load(gains_hbm.at[0], gains_ref),
@@ -427,6 +426,8 @@
 
     odd = lax.rem(lat, 2)
     lat_chip = lat + 1 - 2 * odd
+    lat_cross = lax.rem(lat + lat_count - 1 + 2 * odd, lat_count)
+    lon_cross = (lax.rem(lon + lon_count - 1 + odd, lon_count), lax.rem(lon + odd, lon_count))
     lon_chip = (lax.rem(lon + lon_count - odd, lon_count), lax.rem(lon + 1 - odd, lon_count))
 
     def chip_copy(m, col_half):
@@ -440,6 +441,17 @@
             device_id_type=MESH,
         )
 
+    def cross_copy(m, col_half):
+        piece = 4 - 3 * odd + 2 * col_half
+        return pltpu.make_async_remote_copy(
+            src_ref=done_ref.at[m, piece],
+            dst_ref=home_ref.at[m, piece],
+            send_sem=home_send.at[m, piece],
+            recv_sem=home_recv.at[m, piece],
+            device_id=(0, lat_cross, lon_cross[col_half]),
+            device_id_type=MESH,
+        )
+
     def hand_copy(m, col_half):
         piece = 1 + 3 * odd + 2 * col_half
         return pltpu.make_async_remote_copy(
@@ -461,13 +473,12 @@
             device_id_type=MESH,
         )
 
-    load_fields.wait()
-
     @pl.when(first)
     def _():
-        gather = gather_matrix()
+        gather_ref[...] = gather_matrix()
         for m in range(MICRO):
-            rows = dot(gather, fields_ref[m].reshape(GRID_ROWS, WIDTH))
+            load_fields[m].wait()
+            rows = dot(gather_ref[...], fields_ref[m].reshape(GRID_ROWS, WIDTH))
             refs = [[take_ref] if q in own else [halo_ref] for q in range(PIECES)]
             for window in range(2):
                 pack(rows[window * PACKED : (window + 1) * PACKED], refs, m, window)
@@ -484,6 +495,8 @@
 
     @pl.when(jnp.logical_not(first))
     def _():
+        for copy in load_fields:
+            copy.wait()
         into_ref[...] = owned_matrix()
         last_ref[:, 0 : 2 * TOK] = plain_matrix()
         pl.semaphore_wait(barrier, 1)
@@ -507,21 +520,31 @@
         def _():
             for q in range(PIECES):
                 next_copy(m, q).wait_recv()
-            for col_half in range(2):
-                hand_copy(m, col_half).start()
+
+            @pl.when(m < MICRO - 1)
+            def _():
+                for col_half in range(2):
+                    hand_copy(m, col_half).start()
+
             x_ref[...] = dot(into_ref[...], unpack_both(take_ref, m)).astype(jnp.bfloat16)
 
         x = x_ref[...].astype(jnp.float32)
-        y_ref[...] = block(x, gains_ref, joint_ref, oproj_ref, expand_ref, reduce_ref, bias_ref)
+        projected = project(x, gains_ref, joint_ref)
+        y_ref[...] = finish(x, projected, gains_ref, oproj_ref, expand_ref, reduce_ref, bias_ref)
+        refs = [[done_ref, home_ref] if q in own else [done_ref] for q in range(PIECES)]
 
         @pl.when(first)
         def _():
-            refs = [[done_ref, home_ref] if q in own else [done_ref] for q in range(PIECES)]
             for window in range(2):
-                y = y_ref[window * TOK : (window + 1) * TOK, :]
-                pack(dot(scatter_ref[...], y), refs, m, window)
-            for q in others + own:
-                next_copy(m, q).start()
+                rows = slice(window * TOK, (window + 1) * TOK)
+                pack(dot(scatter_ref[...], y_ref[rows, :]), refs, m, window)
+                for q in (3, 1, 2, 0) if window == 0 else (4, 6, 5, 7):
+                    next_copy(m, q).start()
+            @pl.when(m == MICRO - 1)
+            def _():
+                for col_half in range(2):
+                    cross_copy(m, col_half).start()
+
             for q in (2, 5):
                 home_copy(m, q).start()
             for col_half in range(2):
@@ -551,12 +574,14 @@
                 home_copy(m, q).wait_send()
             for col_half in range(2):
                 chip_copy(m, col_half).wait_send()
+                if m == MICRO - 1:
+                    cross_copy(m, col_half).wait_send()
             for q in range(PIECES):
                 next_copy(m, q).wait_send()
 
     @pl.when(jnp.logical_not(first))
     def _():
-        for m in range(MICRO):
+        for m in range(MICRO - 1):
             for col_half in range(2):
                 hand_copy(m, col_half).wait_send()
 
@@ -581,6 +606,7 @@
         pltpu.VMEM((WIDTH, FF), bf16),
         pltpu.VMEM((FF, WIDTH), bf16),
         pltpu.VMEM((HEADS,) + earth_bias.shape[1:2] + earth_bias.shape[3:], bf16),
+        pltpu.VMEM((2 * PACKED, GRID_ROWS), bf16),
         pltpu.VMEM((2 * TOK, 2 * PACKED), bf16),
         pltpu.VMEM((PACKED, TOK), bf16),
         pltpu.VMEM((GRID_ROWS, 2 * PACKED), bf16),

time: 34.8 us -> 33.3 us (0.957)
  the two profiles are of different devices: /device:TPU:1 before, /device:TPU:2 now
where the time goes in v6:
time: 33.3 us; the launch traced here: 32.9 us
  Pallas kernels  32.1 us (96%)
  local copies, waits for them, and re-layouts  0.76 us (2%)
    pallas_call x1, Pallas kernels, body(): pl.pallas_call(functools.partial(kernel, lat_count, lon_count), out_shape...  32.1 us
    unnamed x1, local copies, waits for them, and re-layouts  0.76 us

profile of v6, /device:TPU:2, one launch (start us, length us, event | category | flops | bytes accessed | tf_op | source)
XLA Modules:
  0.0 32.9 jit_solution(18104683153477882674)
XLA Ops:
  0.0 32.1 %two_blocks.1 = bf16[2,6,12,4,384]{4,3,2,1,0:T(4,128)(2,1)S(1)} custom-call(bf16[2,6,12,4,384]{4,3,2,1,0:T(4,128)(2,1)} %bitcast.7, s32[4,24,384]{2,1,0:T(8,128)} %class_hbm.1, bf16[1,2,384]{2,1,0:T(2,128)(2,1)} %gains_hbm.1, bf16[1,384,1152]{2,1,0:T(8,128)(2,1)} %joint_hbm.1, bf16[1,384,384]{2,1,0:T(8,128)(2,1)} %oproj_hbm.1, ...), custom_call_target="tpu_custom_call" | custom-call | tf_op jit(solution)/shard_map/two_blocks/pallas_call | solution.py:630
  32.2 0.8 %copy.10 = bf16[1,2,4,6,12,384]{5,2,4,3,1,0:T(4,128)(2,1)} copy(bf16[1,2,4,6,12,384]{5,2,4,3,1,0:T(4,128)(2,1)S(1)} %bitcast.5) | data formatting | bytes 884736

commit v7 on v6

--- a/solution.py
+++ b/solution.py
@@ -354,6 +354,7 @@
     home_recv,
     next_send,
     hand_send,
+    ready_sem,
 ):
     sec = lax.axis_index("section")
     lat = lax.axis_index("lat")
@@ -379,12 +380,8 @@
     def _():
         for piece in others:
             pl.semaphore_signal(barrier, inc=1, device_id=(0,) + owner(piece, 1), device_id_type=MESH)
-        pl.semaphore_signal(barrier, inc=1, device_id=(1, lat, lon), device_id_type=MESH)
-
-    @pl.when(jnp.logical_not(first))
-    def _():
         for piece in others + own[:1]:
-            pl.semaphore_signal(barrier, inc=1, device_id=(0,) + owner(piece, 1), device_id_type=MESH)
+            pl.semaphore_signal(barrier, inc=1, device_id=(1,) + owner(piece, 1), device_id_type=MESH)
 
     loads = []
 
@@ -473,19 +470,21 @@
             device_id_type=MESH,
         )
 
+    def send_halo(m):
+        load_fields[m].wait()
+        rows = dot(gather_ref[...], fields_ref[m].reshape(GRID_ROWS, WIDTH))
+        refs = [[take_ref] if q in own else [halo_ref] for q in range(PIECES)]
+        for window in range(2):
+            pack(rows[window * PACKED : (window + 1) * PACKED], refs, m, window)
+        if m == 0:
+            pl.semaphore_wait(barrier, 6)
+        for q in others:
+            halo_copy(m, q).start()
+
     @pl.when(first)
     def _():
         gather_ref[...] = gather_matrix()
-        for m in range(MICRO):
-            load_fields[m].wait()
-            rows = dot(gather_ref[...], fields_ref[m].reshape(GRID_ROWS, WIDTH))
-            refs = [[take_ref] if q in own else [halo_ref] for q in range(PIECES)]
-            for window in range(2):
-                pack(rows[window * PACKED : (window + 1) * PACKED], refs, m, window)
-            if m == 0:
-                pl.semaphore_wait(barrier, 13)
-            for q in others:
-                halo_copy(m, q).start()
+        send_halo(0)
 
     @pl.when(first)
     def _():
@@ -499,13 +498,28 @@
             copy.wait()
         into_ref[...] = owned_matrix()
         last_ref[:, 0 : 2 * TOK] = plain_matrix()
-        pl.semaphore_wait(barrier, 1)
+        pl.semaphore_wait(barrier, 7)
+        for piece in others + own[:1]:
+            pl.semaphore_signal(ready_sem, inc=1, device_id=(0,) + owner(piece, 1), device_id_type=MESH)
 
     for copy in prep:
         copy.wait()
     prepare_bias(first, lat, lon, lat_count, lon_count, class_ref, table_ref, rows_ref, turned_ref, bias_ref)
+
+    @pl.when(first)
+    def _():
+        send_halo(1)
+
     for copy in rest:
         copy.wait()
+
+    def send_rest(m):
+        for q in (1, 6, 0, 7):
+            next_copy(m, q).start()
+        for q in (2, 5):
+            home_copy(m, q).start()
+        for col_half in range(2):
+            chip_copy(m, col_half).start()
 
     def step(m, carry):
         @pl.when(first)
@@ -516,6 +530,10 @@
                 rows = dot(into_ref[0:TOK, 0:PACKED], unpack(take_ref, m, window))
                 x_ref[window * TOK : (window + 1) * TOK, :] = rows.astype(jnp.bfloat16)
 
+            @pl.when(m > 0)
+            def _():
+                send_rest(m - 1)
+
         @pl.when(jnp.logical_not(first))
         def _():
             for q in range(PIECES):
@@ -538,17 +556,19 @@
             for window in range(2):
                 rows = slice(window * TOK, (window + 1) * TOK)
                 pack(dot(scatter_ref[...], y_ref[rows, :]), refs, m, window)
-                for q in (3, 1, 2, 0) if window == 0 else (4, 6, 5, 7):
-                    next_copy(m, q).start()
+
+            @pl.when(m == 0)
+            def _():
+                pl.semaphore_wait(ready_sem, 7)
+
+            for q in (3, 4, 2, 5):
+                next_copy(m, q).start()
+
             @pl.when(m == MICRO - 1)
             def _():
+                send_rest(m)
                 for col_half in range(2):
                     cross_copy(m, col_half).start()
-
-            for q in (2, 5):
-                home_copy(m, q).start()
-            for col_half in range(2):
-                chip_copy(m, col_half).start()
 
         @pl.when(jnp.logical_not(first))
         def _():
@@ -626,6 +646,7 @@
         pltpu.SemaphoreType.DMA((MICRO, PIECES)),
         pltpu.SemaphoreType.DMA((MICRO, PIECES)),
         pltpu.SemaphoreType.DMA((MICRO, 2)),
+        pltpu.SemaphoreType.REGULAR,
     ]
     result = pl.pallas_call(
         functools.partial(kernel, lat_count, lon_count),

time: 33.3 us -> 33.2 us (level)
  no operation moved by 1% of the time
where the time goes in v7:
time: 33.2 us; the launch traced here: 33.1 us
  Pallas kernels  32.4 us (98%)
  local copies, waits for them, and re-layouts  0.76 us (2%)
    pallas_call x1, Pallas kernels, body(): pl.pallas_call(functools.partial(kernel, lat_count, lon_count), out_shape...  32.4 us
    unnamed x1, local copies, waits for them, and re-layouts  0.76 us

profile of v7, /device:TPU:2, one launch (start us, length us, event | category | flops | bytes accessed | tf_op | source)
XLA Modules:
  0.0 33.1 jit_solution(7597871265404282081)
XLA Ops:
  0.0 32.4 %two_blocks.1 = bf16[2,6,12,4,384]{4,3,2,1,0:T(4,128)(2,1)S(1)} custom-call(bf16[2,6,12,4,384]{4,3,2,1,0:T(4,128)(2,1)} %bitcast.7, s32[4,24,384]{2,1,0:T(8,128)} %class_hbm.1, bf16[1,2,384]{2,1,0:T(2,128)(2,1)} %gains_hbm.1, bf16[1,384,1152]{2,1,0:T(8,128)(2,1)} %joint_hbm.1, bf16[1,384,384]{2,1,0:T(8,128)(2,1)} %oproj_hbm.1, ...), custom_call_target="tpu_custom_call" | custom-call | tf_op jit(solution)/shard_map/two_blocks/pallas_call | solution.py:651
  32.4 0.8 %copy.10 = bf16[1,2,4,6,12,384]{5,2,4,3,1,0:T(4,128)(2,1)} copy(bf16[1,2,4,6,12,384]{5,2,4,3,1,0:T(4,128)(2,1)S(1)} %bitcast.5) | data formatting | bytes 884736

commit v8 on v6

--- a/solution.py
+++ b/solution.py
@@ -473,19 +473,21 @@
             device_id_type=MESH,
         )
 
+    def send_halo(m):
+        load_fields[m].wait()
+        rows = dot(gather_ref[...], fields_ref[m].reshape(GRID_ROWS, WIDTH))
+        refs = [[take_ref] if q in own else [halo_ref] for q in range(PIECES)]
+        for window in range(2):
+            pack(rows[window * PACKED : (window + 1) * PACKED], refs, m, window)
+        if m == 0:
+            pl.semaphore_wait(barrier, 13)
+        for q in others:
+            halo_copy(m, q).start()
+
     @pl.when(first)
     def _():
         gather_ref[...] = gather_matrix()
-        for m in range(MICRO):
-            load_fields[m].wait()
-            rows = dot(gather_ref[...], fields_ref[m].reshape(GRID_ROWS, WIDTH))
-            refs = [[take_ref] if q in own else [halo_ref] for q in range(PIECES)]
-            for window in range(2):
-                pack(rows[window * PACKED : (window + 1) * PACKED], refs, m, window)
-            if m == 0:
-                pl.semaphore_wait(barrier, 13)
-            for q in others:
-                halo_copy(m, q).start()
+        send_halo(0)
 
     @pl.when(first)
     def _():
@@ -504,6 +506,11 @@
     for copy in prep:
         copy.wait()
     prepare_bias(first, lat, lon, lat_count, lon_count, class_ref, table_ref, rows_ref, turned_ref, bias_ref)
+
+    @pl.when(first)
+    def _():
+        send_halo(1)
+
     for copy in rest:
         copy.wait()
 
@@ -584,6 +591,20 @@
         for m in range(MICRO - 1):
             for col_half in range(2):
                 hand_copy(m, col_half).wait_send()
+
+
+def write_out(result_ref, out_ref, sem):
+    copies = [
+        pltpu.make_async_copy(
+            result_ref.at[m, pl.ds(3 * half, 3)], out_ref.at[m, pl.ds(3 * half, 3)], sem.at[m, half]
+        )
+        for m in range(MICRO)
+        for half in range(2)
+    ]
+    for copy in copies:
+        copy.start()
+    for copy in copies:
+        copy.wait()
 
 
 def body(
@@ -638,6 +659,15 @@
         ),
         name="two_blocks",
     )(*operands)
+    result = pl.pallas_call(
+        write_out,
+        out_shape=jax.ShapeDtypeStruct(result.shape, bf16),
+        in_specs=[pl.BlockSpec(memory_space=pl.ANY)],
+        out_specs=pl.BlockSpec(memory_space=pl.ANY),
+        scratch_shapes=[pltpu.SemaphoreType.DMA((MICRO, 2))],
+        compiler_params=pltpu.CompilerParams(vmem_limit_bytes=1024 * 1024),
+        name="write_out",
+    )(result)
     return jnp.transpose(result, (0, 3, 1, 2, 4))[None]
 
 

time: 33.3 us -> 33.4 us (level)
  Pallas kernels: 32.1 us -> 33.2 us
  local copies, waits for them, and re-layouts: 0.76 us -> 0 us
    pallas_call x0 -> x1, Pallas kernels: none -> 0.79 us  [body(): pl.pallas_call(write_out, out_shape=jax.ShapeDtypeStruct(result.shape, bf...]
    unnamed x1 -> x0, local copies, waits for them, and re-layouts: 0.76 us -> none
where the time goes in v8:
time: 33.4 us; the launch traced here: 33.2 us
  Pallas kernels  33.2 us (99%)
    pallas_call x1, Pallas kernels, body(): pl.pallas_call(functools.partial(kernel, lat_count, lon_count), out_shape...  32.4 us
    pallas_call x1, Pallas kernels, body(): pl.pallas_call(write_out, out_shape=jax.ShapeDtypeStruct(result.shape, bf...  0.79 us

profile of v8, /device:TPU:2, one launch (start us, length us, event | category | flops | bytes accessed | tf_op | source)
XLA Modules:
  0.0 33.2 jit_solution(12314396266512351367)
XLA Ops:
  0.0 32.4 %two_blocks.1.result_ref = bf16[2,6,12,4,384]{4,3,2,1,0:T(4,128)(2,1)S(1)} custom-call(bf16[2,6,12,4,384]{4,3,2,1,0:T(4,128)(2,1)} %bitcast.6, s32[4,24,384]{2,1,0:T(8,128)} %class_hbm.1, bf16[1,2,384]{2,1,0:T(2,128)(2,1)} %gains_hbm.1, bf16[1,384,1152]{2,1,0:T(8,128)(2,1)} %joint_hbm.1, bf16[1,384,384]{2,1,0:T(8,128)(2,1)} %oproj_hbm.1, ...), custom_call_target="tpu_custom_call" | custom-call | tf_op jit(solution)/shard_map/two_blocks/pallas_call | solution.py:651
  32.4 0.8 %write_out.1 = bf16[2,6,12,4,384]{4,3,2,1,0:T(4,128)(2,1)} custom-call(bf16[2,6,12,4,384]{4,3,2,1,0:T(4,128)(2,1)S(1)} %two_blocks.1.result_ref), custom_call_target="tpu_custom_call" | custom-call | tf_op jit(solution)/shard_map/write_out/pallas_call | solution.py:662
